TPU v7x, 32 devices: a whole 2x2x4 slice. The times are simulated.
32 devices in a mesh: gx: 4 (over y, core), gy: 2 (over x), vert: 4 (over z).
Axes of the slice: x: 2, y: 2, z: 4, core: 2. Of those that a mesh axis runs over, the one named last changes fastest.
Arguments:
- recorded: float32 [4, 512, 128, 256], P('vert', 'gx', 'gy'), may hold values from 0.25 to 4
- psf_taps: float32 [4, 3, 31], P('vert'), may hold values from 0.05 to 1
- estimate: float32 [512, 128, 256], P('gx', ('gy', 'vert')), may hold values from 0.5 to 2
Outputs:
- joined: float32 [512, 128, 256], P('gx', ('gy', 'vert'))
All inputs are finite; a program needn't handle non-finite values.
Results may differ from a plain program's by a relative error of at most 0.0001.
Values sent between devices are 32-bit elements; how exact they have to be, the bound alone decides.
A program may use at most 128 MiB of HBM per device.

v0:
```python
import jax
import jax.numpy as jnp
from jax import lax
from jax.sharding import PartitionSpec as P

ITERS = 2


def extended(x, sides, width):
    for axis, dim in sides:
        size, length = (lax.axis_size(axis), x.shape[dim])
        up = [(i, (i + 1) % size) for i in range(size - 1)]
        down = [(j, i) for i, j in up]
        last = lax.slice_in_dim(x, length - width, length, axis=dim)
        initial = lax.slice_in_dim(x, 0, width, axis=dim)
        before = lax.ppermute(last, axis, up)
        after = lax.ppermute(initial, axis, down)
        x = jnp.concatenate([before, x, after], axis=dim)
    return x


def band(kernel, out_size, in_size, shift_cells, adjoint):
    half_width = (kernel.shape[0] - 1) // 2
    out_index = lax.broadcasted_iota(jnp.int32, (out_size, in_size), 0)
    in_index = lax.broadcasted_iota(jnp.int32, (out_size, in_size), 1)
    offset_cells = in_index - out_index + shift_cells
    if adjoint:
        tap_index = half_width + offset_cells
    else:
        tap_index = half_width - offset_cells
    choose = tap_index[:, :, None] == lax.broadcasted_iota(jnp.int32, (1, 1, kernel.shape[0]), 2)
    return jnp.sum(jnp.where(choose, kernel, jnp.zeros_like(kernel)), axis=2)


def blur_block(volume, kernels, out_x, out_y, shift_cells, adjoint):
    depth_cells = volume.shape[2]
    highest = lax.Precision.HIGHEST
    x_matrix = band(kernels[0], out_x, volume.shape[0], shift_cells, adjoint)
    y_matrix = band(kernels[1], out_y, volume.shape[1], shift_cells, adjoint)
    z_matrix = band(kernels[2], depth_cells, depth_cells, 0, adjoint)
    result = jnp.einsum("pi,ijk->pjk", x_matrix, volume, precision=highest)
    result = jnp.einsum("qj,pjk->pqk", y_matrix, result, precision=highest)
    return jnp.einsum("pqk,rk->pqr", result, z_matrix, precision=highest)


def body(recorded, psf_taps, estimate):
    half_width = (psf_taps.shape[2] - 1) // 2
    view_count = psf_taps.shape[0] * lax.axis_size("vert")
    kernels = psf_taps[0] / jnp.sum(psf_taps[0], axis=1, keepdims=True)
    view_data = recorded[0]
    block_x = view_data.shape[0]
    block_y = view_data.shape[1]
    own_rows = estimate
    for iteration in range(ITERS):
        joined_block = lax.all_gather(own_rows, "vert", axis=1, tiled=True)
        widened = extended(joined_block, (("gx", 0), ("gy", 1)), half_width)
        blurred = blur_block(widened, kernels, block_x, block_y, -half_width, False)
        ratio_wide = extended(view_data / blurred, (("gx", 0), ("gy", 1)), half_width)
        summed = lax.psum_scatter(
            blur_block(ratio_wide, kernels, block_x, block_y, -half_width, True),
            "vert",
            scatter_dimension=1,
            tiled=True,
        )
        own_rows = own_rows * (summed / view_count)
    return own_rows


def solution(mesh):
    in_specs = (P("vert", "gx", "gy", None), P("vert", None, None), P("gx", ("gy", "vert"), None))
    out_specs = P("gx", ("gy", "vert"), None)
    return jax.shard_map(body, mesh=mesh, in_specs=in_specs, out_specs=out_specs, check_vma=False)
```

profile of v0, /device:TPU:0, one launch (start us, length us, event | category | flops | bytes accessed | tf_op | source)
XLA Modules:
  0.0 1118.6 jit_solution(11109354902082627571)
XLA Ops:
  10.7 152.4 %all-gather.3.cloned.1.call-done = f32[128,64,256]{2,0,1:T(8,128)} async-done(((f32[128,16,256]{2,0,1:T(8,128)}), f32[128,64,256]{2,0,1:T(8,128)}) %all-gather.3.cloned.1.call-update) | async-done | bytes 8388624 | tf_op jit(solution)/shard_map/all_gather | solution.py:55
  185.5 39.0 %collective-permute-done.2 = f32[158,15,256]{2,0,1:T(8,128)} collective-permute-done((f32[158,15,256]{2,0,1:T(8,128)}, f32[158,15,256]{2,0,1:T(8,128)}, u32[]{:S(2)}, u32[]{:S(2)}) %collective-permute-start.2) | collective-permute-done | bytes 2426912 | tf_op jit(solution)/shard_map/ppermute | solution.py:16
  224.5 6.2 collective-permute-done.3
  230.7 17.8 %fusion = f32[128,94,256]{2,0,1:T(8,128)} fusion(f32[158,15,256]{2,0,1:T(8,128)} %collective-permute-done.3, f32[15,64,256]{2,0,1:T(8,128)S(1)} %copy.56, f32[128,64,256]{2,0,1:T(8,128)} %all-gather.3.cloned.1.call-done, f32[15,64,256]{2,0,1:T(8,128)S(1)} %copy.55, f32[158,15,256]{2,0,1:T(8,128)} %collective-permute-done.2, f32[128,158]{0,1:T(8,128)S(1)} %get-tuple-element.10), kind=kOutput, calls=%fused_computation | convolution fusion | flops 5855252480 | bytes 27610112 | tf_op jit(solution)/shard_map/pi,ijk->pjk/dot_general | solution.py:41
  248.5 22.5 %fusion.56 = f32[128,64,256]{2,1,0:T(8,128)S(1)} fusion(f32[128,94,256]{2,0,1:T(8,128)} %fusion, f32[64,94]{1,0:T(8,128)S(1)} %get-tuple-element.8), kind=kOutput, calls=%fused_computation.62 | convolution fusion | flops 2365587456 | bytes 20733440 | tf_op jit(solution)/shard_map/qj,pjk->pqk/dot_general | solution.py:42
  271.0 16.7 %bitcast_divide_fusion.1 = f32[128,64,256]{2,0,1:T(8,128)S(1)} fusion(f32[1,128,64,256]{3,2,1,0:T(8,128)} %param.3, f32[128,64,256]{2,1,0:T(8,128)S(1)} %fusion.56, f32[256,256]{1,0:T(8,128)S(1)} %get-tuple-element.6), kind=kOutput, calls=%fused_computation.49 | convolution fusion | flops 6444548096 | bytes 25427968 | tf_op jit(solution)/shard_map/pqk,rk->pqr/dot_general | solution.py:43
  290.3 11.4 %collective-permute-start.4 = (f32[15,64,256]{2,1,0:T(8,128)S(1)}, f32[15,64,256]{2,1,0:T(8,128)S(1)}, u32[]{:S(2)}, u32[]{:S(2)}) collective-permute-start(f32[15,64,256]{2,1,0:T(8,128)S(1)} %copy.59), channel_id=1, source_target_pairs={{0,8},{8,16},{16,24},{1,9},{9,17},{17,25},{2,10},{10,18},{18,26},{... | collective-permute-start | bytes 2949128 | tf_op jit(solution)/shard_map/ppermute | solution.py:16
  308.3 42.6 %collective-permute-done.6 = f32[158,15,256]{2,0,1:T(8,128)S(1)} collective-permute-done((f32[158,15,256]{2,0,1:T(8,128)S(1)}, f32[158,15,256]{2,0,1:T(8,128)S(1)}, u32[]{:S(2)}, u32[]{:S(2)}) %collective-permute-start.6) | collective-permute-done | bytes 2426912 | tf_op jit(solution)/shard_map/ppermute | solution.py:16
  357.2 17.7 %fusion.10 = f32[128,94,256]{2,0,1:T(8,128)} fusion(f32[158,15,256]{2,0,1:T(8,128)} %copy-done.7, f32[15,64,256]{2,0,1:T(8,128)S(1)} %copy.62, f32[128,64,256]{2,0,1:T(8,128)} %copy-done.4, f32[15,64,256]{2,0,1:T(8,128)S(1)} %copy.61, f32[158,15,256]{2,0,1:T(8,128)S(1)} %collective-permute-done.6, f32[128,158]{0,1:T(8,128)S(1)} %get-tuple-element.9), kind=kOutput, calls=%fused_computation.10 | convolution fusion | flops 5855252480 | bytes 27610112 | tf_op jit(solution)/shard_map/pi,ijk->pjk/dot_general | solution.py:41
  374.9 22.8 %fusion.59 = f32[128,64,256]{2,1,0:T(8,128)S(1)} fusion(f32[128,94,256]{2,0,1:T(8,128)} %fusion.10, f32[64,94]{1,0:T(8,128)S(1)} %get-tuple-element.7), kind=kOutput, calls=%fused_computation.63 | convolution fusion | flops 2365587456 | bytes 20733440 | tf_op jit(solution)/shard_map/qj,pjk->pqk/dot_general | solution.py:42
  397.7 12.0 %fusion.52 = f32[128,64,256]{2,0,1:T(8,128)} fusion(f32[128,64,256]{2,1,0:T(8,128)S(1)} %fusion.59, f32[256,256]{1,0:T(8,128)S(1)} %get-tuple-element.5), kind=kOutput, calls=%fused_computation.54 | convolution fusion | flops 6442450944 | bytes 17039360 | tf_op jit(solution)/shard_map/pqk,rk->pqr/dot_general | solution.py:43
  409.8 150.6 %reduce-scatter.3.cloned.1.call-done = f32[128,16,256]{2,0,1:T(8,128)} async-done(((f32[128,64,256]{2,0,1:T(8,128)}), f32[128,16,256]{2,0,1:T(8,128)}) %reduce-scatter.3.cloned.1.call-update) | async-done | bytes 2097168 | tf_op jit(solution)/shard_map/reduce_scatter | solution.py:59
  564.7 150.4 %all-gather.5.cloned.1.call-done = f32[128,64,256]{2,0,1:T(8,128)} async-done(((f32[128,16,256]{2,0,1:T(8,128)}), f32[128,64,256]{2,0,1:T(8,128)}) %all-gather.5.cloned.1.call-update) | async-done | bytes 8388624 | tf_op jit(solution)/shard_map/all_gather | solution.py:55
  731.0 43.0 %collective-permute-done.10 = f32[158,15,256]{2,0,1:T(8,128)S(1)} collective-permute-done((f32[158,15,256]{2,0,1:T(8,128)S(1)}, f32[158,15,256]{2,0,1:T(8,128)S(1)}, u32[]{:S(2)}, u32[]{:S(2)}) %collective-permute-start.10) | collective-permute-done | bytes 2426912 | tf_op jit(solution)/shard_map/ppermute | solution.py:16
  778.9 17.9 %fusion.20 = f32[128,94,256]{2,0,1:T(8,128)} fusion(f32[158,15,256]{2,0,1:T(8,128)} %collective-permute-done.11, f32[15,64,256]{2,0,1:T(8,128)S(1)} %copy.69, f32[128,64,256]{2,0,1:T(8,128)} %all-gather.5.cloned.1.call-done, f32[15,64,256]{2,0,1:T(8,128)S(1)} %copy.68, f32[158,15,256]{2,0,1:T(8,128)S(1)} %collective-permute-done.10, ...), kind=kOutput, calls=%fused_computation.20 | convolution fusion | flops 5855252480 | bytes 27610112 | tf_op jit(solution)/shard_map/pi,ijk->pjk/dot_general | solution.py:41
  796.8 22.4 %fusion.62 = f32[128,64,256]{2,1,0:T(8,128)S(1)} fusion(f32[128,94,256]{2,0,1:T(8,128)} %fusion.20, f32[64,94]{1,0:T(8,128)S(1)} %get-tuple-element.8), kind=kOutput, calls=%fused_computation.64 | convolution fusion | flops 2365587456 | bytes 20733440 | tf_op jit(solution)/shard_map/qj,pjk->pqk/dot_general | solution.py:42
  819.3 16.4 %bitcast_divide_fusion = f32[128,64,256]{2,0,1:T(8,128)S(1)} fusion(f32[1,128,64,256]{3,2,1,0:T(8,128)} %param.3, f32[128,64,256]{2,1,0:T(8,128)S(1)} %fusion.62, f32[256,256]{1,0:T(8,128)S(1)} %get-tuple-element.6), kind=kOutput, calls=%fused_computation.48 | convolution fusion | flops 6444548096 | bytes 25427968 | tf_op jit(solution)/shard_map/pqk,rk->pqr/dot_general | solution.py:43
  838.4 11.4 %collective-permute-start.12 = (f32[15,64,256]{2,1,0:T(8,128)S(1)}, f32[15,64,256]{2,1,0:T(8,128)S(1)}, u32[]{:S(2)}, u32[]{:S(2)}) collective-permute-start(f32[15,64,256]{2,1,0:T(8,128)S(1)} %copy.72), channel_id=1, source_target_pairs={{0,8},{8,16},{16,24},{1,9},{9,17},{17,25},{2,10},{10,18},{18,26},{... | collective-permute-start | bytes 2949128 | tf_op jit(solution)/shard_map/ppermute | solution.py:16
  856.2 42.6 %collective-permute-done.14 = f32[158,15,256]{2,0,1:T(8,128)S(1)} collective-permute-done((f32[158,15,256]{2,0,1:T(8,128)S(1)}, f32[158,15,256]{2,0,1:T(8,128)S(1)}, u32[]{:S(2)}, u32[]{:S(2)}) %collective-permute-start.14) | collective-permute-done | bytes 2426912 | tf_op jit(solution)/shard_map/ppermute | solution.py:16
  898.8 4.9 collective-permute-done.15
  903.8 17.8 %fusion.30 = f32[128,94,256]{2,0,1:T(8,128)} fusion(f32[158,15,256]{2,0,1:T(8,128)} %collective-permute-done.15, f32[15,64,256]{2,0,1:T(8,128)S(1)} %copy.75, f32[128,64,256]{2,0,1:T(8,128)} %copy-done.3, f32[15,64,256]{2,0,1:T(8,128)S(1)} %copy.74, f32[158,15,256]{2,0,1:T(8,128)S(1)} %collective-permute-done.14, f32[128,158]{0,1:T(8,128)S(1)} %get-tuple-element.9), kind=kOutput, calls=%fused_computation.30 | convolution fusion | flops 5855252480 | bytes 27610112 | tf_op jit(solution)/shard_map/pi,ijk->pjk/dot_general | solution.py:41
  921.5 23.3 %fusion.65 = f32[128,64,256]{2,1,0:T(8,128)S(1)} fusion(f32[128,94,256]{2,0,1:T(8,128)} %fusion.30, f32[64,94]{1,0:T(8,128)S(1)} %get-tuple-element.7), kind=kOutput, calls=%fused_computation.65 | convolution fusion | flops 2365587456 | bytes 20733440 | tf_op jit(solution)/shard_map/qj,pjk->pqk/dot_general | solution.py:42
  944.8 12.0 %fusion.48 = f32[128,64,256]{2,0,1:T(8,128)} fusion(f32[128,64,256]{2,1,0:T(8,128)S(1)} %fusion.65, f32[256,256]{1,0:T(8,128)S(1)} %get-tuple-element.5), kind=kOutput, calls=%fused_computation.50 | convolution fusion | flops 6442450944 | bytes 17039360 | tf_op jit(solution)/shard_map/pqk,rk->pqr/dot_general | solution.py:43
  956.8 150.6 %reduce-scatter.5.cloned.1.call-done = f32[128,16,256]{2,0,1:T(8,128)} async-done(((f32[128,64,256]{2,0,1:T(8,128)}), f32[128,16,256]{2,0,1:T(8,128)}) %reduce-scatter.5.cloned.1.call-update) | async-done | bytes 2097168 | tf_op jit(solution)/shard_map/reduce_scatter | solution.py:59
  (85 shorter events, 80.3 us)
Async XLA Ops:
  6.5 156.6 %all-gather.3.cloned.1.call-start = ((), (), s32[]{:S(2)}) async-start(), calls=%async_computation.2 | async-start | bytes 10485760 | tf_op jit(solution)/shard_map/all_gather | solution.py:55
  10.7 549.8 %reduce-scatter.3.cloned.1.call-start = ((), (), s32[]{:S(2)}) async-start(), calls=%async_computation.3 | async-start | bytes 10485760 | tf_op jit(solution)/shard_map/reduce_scatter | solution.py:59
  165.7 5.1 collective-permute-start.1
  167.7 5.2 collective-permute-start
  176.3 48.2 %collective-permute-start.2 = (f32[158,15,256]{2,0,1:T(8,128)}, f32[158,15,256]{2,0,1:T(8,128)}, u32[]{:S(2)}, u32[]{:S(2)}) collective-permute-start(f32[158,15,256]{2,0,1:T(8,128)} %get-tuple-element.17), channel_id=1, source_target_pairs={{0,4},{1,5},{2,6},{3,7},{8,12},{9,13},{10,14},{11,15},{16,20},{17,... | collective-permute-start | bytes 7280648 | tf_op jit(solution)/shard_map/ppermute | solution.py:16
  181.2 49.5 %collective-permute-start.3 = (f32[158,15,256]{2,0,1:T(8,128)}, f32[158,15,256]{2,0,1:T(8,128)}, u32[]{:S(2)}, u32[]{:S(2)}) collective-permute-start(f32[158,15,256]{2,0,1:T(8,128)} %get-tuple-element.18), channel_id=1, source_target_pairs={{4,0},{5,1},{6,2},{7,3},{12,8},{13,9},{14,10},{15,11},{20,16},{21,... | collective-permute-start | bytes 7280648 | tf_op jit(solution)/shard_map/ppermute | solution.py:17
  287.7 17.4 %copy-start.4 = (f32[128,64,256]{2,0,1:T(8,128)}, f32[128,64,256]{2,0,1:T(8,128)S(1)}, u32[]{:S(2)}) copy-start(f32[128,64,256]{2,0,1:T(8,128)S(1)} %bitcast_divide_fusion.1) | copy-start | bytes 25165828
  288.5 13.3 %collective-permute-start.5 = (f32[15,64,256]{2,1,0:T(8,128)S(1)}, f32[15,64,256]{2,1,0:T(8,128)S(1)}, u32[]{:S(2)}, u32[]{:S(2)}) collective-permute-start(f32[15,64,256]{2,1,0:T(8,128)S(1)} %copy.60), channel_id=1, source_target_pairs={{8,0},{16,8},{24,16},{9,1},{17,9},{25,17},{10,2},{18,10},{26,18},{... | collective-permute-start | bytes 2949128 | tf_op jit(solution)/shard_map/ppermute | solution.py:17
  290.3 13.5 %collective-permute-start.4 = (f32[15,64,256]{2,1,0:T(8,128)S(1)}, f32[15,64,256]{2,1,0:T(8,128)S(1)}, u32[]{:S(2)}, u32[]{:S(2)}) collective-permute-start(f32[15,64,256]{2,1,0:T(8,128)S(1)} %copy.59), channel_id=1, source_target_pairs={{0,8},{8,16},{16,24},{1,9},{9,17},{17,25},{2,10},{10,18},{18,26},{... | collective-permute-start | bytes 2949128 | tf_op jit(solution)/shard_map/ppermute | solution.py:16
  305.1 45.8 %collective-permute-start.6 = (f32[158,15,256]{2,0,1:T(8,128)S(1)}, f32[158,15,256]{2,0,1:T(8,128)S(1)}, u32[]{:S(2)}, u32[]{:S(2)}) collective-permute-start(f32[158,15,256]{2,0,1:T(8,128)S(1)} %get-tuple-element.15), channel_id=1, source_target_pairs={{0,4},{1,5},{2,6},{3,7},{8,12},{9,13},{10,14},{11,15},{16,20},{17,... | collective-permute-start | bytes 7280648 | tf_op jit(solution)/shard_map/ppermute | solution.py:16
  307.0 48.7 %collective-permute-start.7 = (f32[158,15,256]{2,0,1:T(8,128)S(1)}, f32[158,15,256]{2,0,1:T(8,128)S(1)}, u32[]{:S(2)}, u32[]{:S(2)}) collective-permute-start(f32[158,15,256]{2,0,1:T(8,128)S(1)} %get-tuple-element.16), channel_id=1, source_target_pairs={{4,0},{5,1},{6,2},{7,3},{12,8},{13,9},{14,10},{15,11},{20,16},{21,... | collective-permute-start | bytes 7280648 | tf_op jit(solution)/shard_map/ppermute | solution.py:17
  409.8 150.7 %copy-start.5 = (f32[128,16,256]{2,1,0:T(8,128)S(1)}, f32[128,16,256]{2,1,0:T(8,128)}, u32[]{:S(2)}) copy-start(f32[128,16,256]{2,1,0:T(8,128)} %param.5) | copy-start | bytes 6291460
  409.8 305.4 %all-gather.5.cloned.1.call-start = ((), (), s32[]{:S(2)}) async-start(), calls=%async_computation.4 | async-start | bytes 10485760 | tf_op jit(solution)/shard_map/all_gather | solution.py:55
  564.7 542.8 %reduce-scatter.5.cloned.1.call-start = ((), (), s32[]{:S(2)}) async-start(), calls=%async_computation.5 | async-start | bytes 10485760 | tf_op jit(solution)/shard_map/reduce_scatter | solution.py:59
  717.6 5.1 collective-permute-start.9
  719.6 5.2 collective-permute-start.8
  726.1 47.9 %collective-permute-start.10 = (f32[158,15,256]{2,0,1:T(8,128)S(1)}, f32[158,15,256]{2,0,1:T(8,128)S(1)}, u32[]{:S(2)}, u32[]{:S(2)}) collective-permute-start(f32[158,15,256]{2,0,1:T(8,128)S(1)} %get-tuple-element.13), channel_id=1, source_target_pairs={{0,4},{1,5},{2,6},{3,7},{8,12},{9,13},{10,14},{11,15},{16,20},{17,... | collective-permute-start | bytes 7280648 | tf_op jit(solution)/shard_map/ppermute | solution.py:16
  729.7 49.3 %collective-permute-start.11 = (f32[158,15,256]{2,0,1:T(8,128)S(1)}, f32[158,15,256]{2,0,1:T(8,128)}, u32[]{:S(2)}, u32[]{:S(2)}) collective-permute-start(f32[158,15,256]{2,0,1:T(8,128)S(1)} %get-tuple-element.14), channel_id=1, source_target_pairs={{4,0},{5,1},{6,2},{7,3},{12,8},{13,9},{14,10},{15,11},{20,16},{21,... | collective-permute-start | bytes 7280648 | tf_op jit(solution)/shard_map/ppermute | solution.py:17
  835.7 17.4 %copy-start.3 = (f32[128,64,256]{2,0,1:T(8,128)}, f32[128,64,256]{2,0,1:T(8,128)S(1)}, u32[]{:S(2)}) copy-start(f32[128,64,256]{2,0,1:T(8,128)S(1)} %bitcast_divide_fusion) | copy-start | bytes 25165828
  836.5 13.3 %collective-permute-start.13 = (f32[15,64,256]{2,1,0:T(8,128)S(1)}, f32[15,64,256]{2,1,0:T(8,128)S(1)}, u32[]{:S(2)}, u32[]{:S(2)}) collective-permute-start(f32[15,64,256]{2,1,0:T(8,128)S(1)} %copy.73), channel_id=1, source_target_pairs={{8,0},{16,8},{24,16},{9,1},{17,9},{25,17},{10,2},{18,10},{26,18},{... | collective-permute-start | bytes 2949128 | tf_op jit(solution)/shard_map/ppermute | solution.py:17
  838.4 13.5 %collective-permute-start.12 = (f32[15,64,256]{2,1,0:T(8,128)S(1)}, f32[15,64,256]{2,1,0:T(8,128)S(1)}, u32[]{:S(2)}, u32[]{:S(2)}) collective-permute-start(f32[15,64,256]{2,1,0:T(8,128)S(1)} %copy.72), channel_id=1, source_target_pairs={{0,8},{8,16},{16,24},{1,9},{9,17},{17,25},{2,10},{10,18},{18,26},{... | collective-permute-start | bytes 2949128 | tf_op jit(solution)/shard_map/ppermute | solution.py:16
  853.1 45.7 %collective-permute-start.14 = (f32[158,15,256]{2,0,1:T(8,128)S(1)}, f32[158,15,256]{2,0,1:T(8,128)S(1)}, u32[]{:S(2)}, u32[]{:S(2)}) collective-permute-start(f32[158,15,256]{2,0,1:T(8,128)S(1)} %get-tuple-element.11), channel_id=1, source_target_pairs={{0,4},{1,5},{2,6},{3,7},{8,12},{9,13},{10,14},{11,15},{16,20},{17,... | collective-permute-start | bytes 7280648 | tf_op jit(solution)/shard_map/ppermute | solution.py:16
  854.9 48.8 %collective-permute-start.15 = (f32[158,15,256]{2,0,1:T(8,128)S(1)}, f32[158,15,256]{2,0,1:T(8,128)}, u32[]{:S(2)}, u32[]{:S(2)}) collective-permute-start(f32[158,15,256]{2,0,1:T(8,128)S(1)} %get-tuple-element.12), channel_id=1, source_target_pairs={{4,0},{5,1},{6,2},{7,3},{12,8},{13,9},{14,10},{15,11},{20,16},{21,... | collective-permute-start | bytes 7280648 | tf_op jit(solution)/shard_map/ppermute | solution.py:17
  956.8 150.7 %copy-start = (f32[128,16,256]{2,0,1:T(8,128)S(1)}, f32[128,16,256]{2,0,1:T(8,128)}, u32[]{:S(2)}) copy-start(f32[128,16,256]{2,0,1:T(8,128)} %multiply_multiply_fusion.1) | copy-start | bytes 6291460
  (4 other events, 33.4 us)
Sparse Core Ops, SparseCore 0:
  10.8 152.3 all-gather.2
  409.9 150.4 reduce-scatter.2
  564.8 150.3 all-gather.4
  956.9 150.4 reduce-scatter.4
where the time goes:
time: 1120 us
  waiting for transfers between devices  798 us (71%)
  matrix products  219 us (20%)
  starting transfers between devices  52 us (5%)
  local copies, waits for them, and re-layouts  21.5 us (2%)
  between operations  13.8 us (1%)
  other arithmetic  13.7 us (1%)
    all_gather x2, waiting for transfers between devices, body(): joined_block = lax.all_gather(own_rows, 'vert', axis=1, tiled=True)  303 us
    reduce_scatter x2, waiting for transfers between devices, body(): lax.psum_scatter(blur_block(ratio_wide, kernels, block_x, block_y, -half_...  301 us
    ppermute x8, waiting for transfers between devices, extended(): before = lax.ppermute(last, axis, up)  173 us
    dot_general x4, matrix products, blur_block(): result = jnp.einsum('qj,pjk->pqk', y_matrix, result, precision=highest)  91 us
    dot_general x4, matrix products, blur_block(): result = jnp.einsum('pi,ijk->pjk', x_matrix, volume, precision=highest)  71.2 us
    dot_general x4, matrix products, blur_block(): return jnp.einsum('pqk,rk->pqr', result, z_matrix, precision=highest)  57.2 us
    ppermute x8, starting transfers between devices, extended(): before = lax.ppermute(last, axis, up)  41 us
  transfers between devices with their start and end apart: 20, of which 16 were waited for; matrix products, arithmetic and copies ran while one was open for 1% of the time, Pallas kernels for 0%

commit v1 on v0

v1 whole, which is shorter than its diff:
```python
import jax
import jax.numpy as jnp
from jax import lax
from jax.sharding import PartitionSpec as P

ITERS = 2
PIECES = 2


def halo(x, axis, dim, width):
    size, length = (lax.axis_size(axis), x.shape[dim])
    up = [(i, i + 1) for i in range(size - 1)]
    down = [(i + 1, i) for i in range(size - 1)]
    before = lax.ppermute(lax.slice_in_dim(x, length - width, length, axis=dim), axis, up)
    after = lax.ppermute(lax.slice_in_dim(x, 0, width, axis=dim), axis, down)
    return before, after


def band(kernel, out_size, in_size, shift_cells, adjoint):
    half_width = (kernel.shape[0] - 1) // 2
    out_index = lax.broadcasted_iota(jnp.int32, (out_size, in_size), 0)
    in_index = lax.broadcasted_iota(jnp.int32, (out_size, in_size), 1)
    offset_cells = in_index - out_index + shift_cells
    if adjoint:
        tap_index = half_width + offset_cells
    else:
        tap_index = half_width - offset_cells
    choose = tap_index[:, :, None] == lax.broadcasted_iota(jnp.int32, (1, 1, kernel.shape[0]), 2)
    return jnp.sum(jnp.where(choose, kernel, jnp.zeros_like(kernel)), axis=2)


def body(recorded, psf_taps, estimate):
    m = (psf_taps.shape[2] - 1) // 2
    view_count = psf_taps.shape[0] * lax.axis_size("vert")
    kernels = psf_taps[0] / jnp.sum(psf_taps[0], axis=1, keepdims=True)
    view_data = recorded[0]
    bx, bz, by = view_data.shape
    rows = bx // PIECES
    high = lax.Precision.HIGH
    mats = []
    for adjoint in (False, True):
        mats.append((
            band(kernels[0], bx, bx + 2 * m, -m, adjoint),
            band(kernels[1], bz, bz + 2 * m, -m, adjoint),
            band(kernels[2], by, by, 0, adjoint),
        ))
    order = []
    for i in range((PIECES + 1) // 2):
        order += [i] if i == PIECES - 1 - i else [i, PIECES - 1 - i]

    def dims12(piece, zmat, ymat):
        before, after = halo(piece, "gy", 1, m)
        wide = jnp.concatenate([before, piece, after], axis=1)
        out = jnp.einsum("qj,pjk->pqk", zmat, wide, precision=high)
        return jnp.einsum("pqk,rk->pqr", out, ymat, precision=high)

    own = [estimate[i * rows:(i + 1) * rows] for i in range(PIECES)]
    for iteration in range(ITERS):
        fx, fz, fy = mats[0]
        blur = [None] * PIECES
        last = None
        for i in order:
            src = own[i]
            if last is not None:
                src, last = lax.optimization_barrier((src, last))
            last = lax.all_gather(src, "vert", axis=1, tiled=True)
            blur[i] = last
        blur = [dims12(b, fz, fy) for b in blur]
        nx_before, nx_after = edge_halo(blur, m)
        wide = jnp.concatenate([nx_before] + blur + [nx_after], axis=0)
        blurred = jnp.einsum("pi,ijk->pjk", fx, wide, precision=high)
        ratio = view_data / blurred
        ax, az, ay = mats[1]
        before, after = halo(ratio, "gx", 0, m)
        wide = jnp.concatenate([before, ratio, after], axis=0)
        new = [None] * PIECES
        last = None
        for i in order:
            lo = i * rows
            part = jnp.einsum("pi,ijk->pjk", ax[lo:lo + rows, lo:lo + rows + 2 * m], wide[lo:lo + rows + 2 * m], precision=high)
            corr = dims12(part, az, ay)
            if last is not None:
                corr, last = lax.optimization_barrier((corr, last))
            last = lax.psum_scatter(corr, "vert", scatter_dimension=1, tiled=True)
            new[i] = own[i] * (last / view_count)
        own = new
    return jnp.concatenate(own, axis=0)


def edge_halo(parts, m):
    size = lax.axis_size("gx")
    before = lax.ppermute(parts[-1][-m:], "gx", [(i, i + 1) for i in range(size - 1)])
    after = lax.ppermute(parts[0][:m], "gx", [(i + 1, i) for i in range(size - 1)])
    return before, after


def solution(mesh):
    in_specs = (P("vert", "gx", "gy", None), P("vert", None, None), P("gx", ("gy", "vert"), None))
    out_specs = P("gx", ("gy", "vert"), None)
    return jax.shard_map(body, mesh=mesh, in_specs=in_specs, out_specs=out_specs, check_vma=False)
```

time: 1120 us -> 909 us (0.81)
  waiting for transfers between devices: 798 us -> 648 us
  matrix products: 219 us -> 108 us
  starting transfers between devices: 52 us -> 79.4 us
    dot_general x12 -> x22, matrix products: 219 us -> 108 us  [the longest x8 35.5 us: dims12(): out = jnp.einsum('qj,pjk->pqk', zmat, wide, precision=high)]
    ppermute x16 -> x24, waiting for transfers between devices: 194 us -> 112 us  [the longest x10 62.6 us: halo(): after = lax.ppermute(lax.slice_in_dim(x, 0, width, axis=dim), axis, down)]
    reduce_scatter x2 -> x4, waiting for transfers between devices: 301 us -> 234 us  [body(): last = lax.psum_scatter(corr, 'vert', scatter_dimension=1, tiled=True)]
    ppermute x16 -> x24, starting transfers between devices: 51.8 us -> 78.5 us  [the longest x10 59.6 us: halo(): lax.ppermute(lax.slice_in_dim(x, length - width, length, axis=dim), axis,...]
    slice x12 -> x27, local copies, waits for them, and re-layouts: 8.71 us -> 20.6 us  [the longest x16 12.8 us: halo(): lax.slice_in_dim(x, length - width, length, axis=dim)]
    all_gather x2 -> x4, waiting for transfers between devices: 303 us -> 302 us  [body(): last = lax.all_gather(src, 'vert', axis=1, tiled=True)]
  transfers between devices with their start and end apart: 20 -> 32, of which waited for: 16 -> 26; matrix products, arithmetic and copies ran while one was open for 1% -> 9% of each run, Pallas kernels for 0% -> 0%
where the time goes in v1:
time: 909 us; the launch traced here: 900 us
  waiting for transfers between devices  648 us (71%)
  matrix products  108 us (12%)
  starting transfers between devices  79.4 us (9%)
  local copies, waits for them, and re-layouts  31.1 us (3%)
  other arithmetic  19 us (2%)
  between operations  14.5 us (2%)
    all_gather x4, waiting for transfers between devices, body(): last = lax.all_gather(src, 'vert', axis=1, tiled=True)  302 us
    reduce_scatter x4, waiting for transfers between devices, body(): last = lax.psum_scatter(corr, 'vert', scatter_dimension=1, tiled=True)  234 us
    ppermute x10, waiting for transfers between devices, halo(): after = lax.ppermute(lax.slice_in_dim(x, 0, width, axis=dim), axis, down)  62.6 us
    ppermute x10, starting transfers between devices, halo(): lax.ppermute(lax.slice_in_dim(x, length - width, length, axis=dim), axis,...  59.6 us
    ppermute x10, waiting for transfers between devices, halo(): lax.ppermute(lax.slice_in_dim(x, length - width, length, axis=dim), axis,...  46.7 us
    dot_general x8, matrix products, dims12(): out = jnp.einsum('qj,pjk->pqk', zmat, wide, precision=high)  35.5 us
    dot_general x2, matrix products, body(): blurred = jnp.einsum('pi,ijk->pjk', fx, wide, precision=high)  33.5 us
    dot_general x8, matrix products, dims12(): return jnp.einsum('pqk,rk->pqr', out, ymat, precision=high)  22.9 us
  transfers between devices with their start and end apart: 32, of which 26 were waited for; matrix products, arithmetic and copies ran while one was open for 9% of the time, Pallas kernels for 0%

profile of v1, /device:TPU:0, one launch (start us, length us, event | category | flops | bytes accessed | tf_op | source)
XLA Modules:
  0.0 899.8 jit_solution(12214630533791276856)
XLA Ops:
  9.7 83.6 %all-gather.5.cloned.1.call-done = f32[64,64,256]{2,1,0:T(8,128)} async-done(((f32[64,16,256]{2,1,0:T(8,128)}), f32[64,64,256]{2,1,0:T(8,128)}) %all-gather.5.cloned.1.call-update) | async-done | bytes 4194320 | tf_op jit(solution)/shard_map/all_gather | solution.py:66
  98.7 6.5 collective-permute-start.3
  106.8 67.3 %all-gather.7.cloned.1.call-done = f32[64,64,256]{2,1,0:T(8,128)} async-done(((f32[64,16,256]{2,1,0:T(8,128)}), f32[64,64,256]{2,1,0:T(8,128)}) %all-gather.7.cloned.1.call-update) | async-done | bytes 4194320 | tf_op jit(solution)/shard_map/all_gather | solution.py:66
  193.7 8.9 collective-permute-done.1
  215.3 16.7 %bitcast_divide_fusion.1 = f32[128,64,256]{2,0,1:T(8,128)S(1)} fusion(f32[1,128,64,256]{3,2,1,0:T(8,128)} %param.3, f32[158,64,256]{2,1,0:T(8,128)S(1)} %pad_maximum_fusion, f32[128,158]{0,1:T(8,128)} %get-tuple-element.18), kind=kOutput, calls=%fused_computation.7 | convolution fusion | flops 1990197248 | bytes 27212800 | tf_op jit(solution)/shard_map/pi,ijk->pjk/dot_general | solution.py:71
  232.9 13.4 %collective-permute-start.6 = (f32[15,64,256]{2,1,0:T(8,128)S(1)}, f32[15,64,256]{2,1,0:T(8,128)S(1)}, u32[]{:S(2)}, u32[]{:S(2)}) collective-permute-start(f32[15,64,256]{2,1,0:T(8,128)S(1)} %copy.45), channel_id=1, source_target_pairs={{0,8},{8,16},{16,24},{1,9},{9,17},{17,25},{2,10},{10,18},{18,26},{... | collective-permute-start | bytes 2949128 | tf_op jit(solution)/shard_map/ppermute | solution.py:14
  257.4 10.3 %collective-permute-done.7 = f32[64,15,256]{2,0,1:T(8,128)S(1)} collective-permute-done((f32[64,15,256]{2,0,1:T(8,128)S(1)}, f32[64,15,256]{2,0,1:T(8,128)S(1)}, u32[]{:S(2)}, u32[]{:S(2)}) %collective-permute-start.7) | collective-permute-done | bytes 983072 | tf_op jit(solution)/shard_map/ppermute | solution.py:14
  273.3 5.8 fusion.42
  285.1 12.6 %collective-permute-done.9 = f32[15,64,256]{2,1,0:T(8,128)S(1)} collective-permute-done((f32[15,64,256]{2,1,0:T(8,128)S(1)}, f32[15,64,256]{2,1,0:T(8,128)S(1)}, u32[]{:S(2)}, u32[]{:S(2)}) %collective-permute-start.9) | collective-permute-done | bytes 983072 | tf_op jit(solution)/shard_map/ppermute | solution.py:15
  306.2 10.2 %collective-permute-done.10 = f32[64,15,256]{2,0,1:T(8,128)S(1)} collective-permute-done((f32[64,15,256]{2,0,1:T(8,128)S(1)}, f32[64,15,256]{2,0,1:T(8,128)S(1)}, u32[]{:S(2)}, u32[]{:S(2)}) %collective-permute-start.10) | collective-permute-done | bytes 983072 | tf_op jit(solution)/shard_map/ppermute | solution.py:14
  321.7 5.8 fusion.40
  331.3 38.1 %reduce-scatter.5.cloned.1.call-done = f32[64,16,256]{2,1,0:T(8,128)} async-done(((f32[64,64,256]{2,1,0:T(8,128)}), f32[64,16,256]{2,1,0:T(8,128)}) %reduce-scatter.5.cloned.1.call-update) | async-done | bytes 1048592 | tf_op jit(solution)/shard_map/reduce_scatter | solution.py:84
  369.5 79.5 %reduce-scatter.7.cloned.1.call-done = f32[64,16,256]{2,1,0:T(8,128)} async-done(((f32[64,64,256]{2,1,0:T(8,128)}), f32[64,16,256]{2,1,0:T(8,128)}) %reduce-scatter.7.cloned.1.call-update) | async-done | bytes 1048592 | tf_op jit(solution)/shard_map/reduce_scatter | solution.py:84
  452.4 81.4 %all-gather.9.cloned.1.call-done = f32[64,64,256]{2,1,0:T(8,128)} async-done(((f32[64,16,256]{2,1,0:T(8,128)}), f32[64,64,256]{2,1,0:T(8,128)}) %all-gather.9.cloned.1.call-update) | async-done | bytes 4194320 | tf_op jit(solution)/shard_map/all_gather | solution.py:66
  544.8 69.8 %all-gather.11.cloned.1.call-done = f32[64,64,256]{2,1,0:T(8,128)} async-done(((f32[64,16,256]{2,1,0:T(8,128)}), f32[64,64,256]{2,1,0:T(8,128)}) %all-gather.11.cloned.1.call-update) | async-done | bytes 4194320 | tf_op jit(solution)/shard_map/all_gather | solution.py:66
  632.4 10.0 %collective-permute-done.13 = f32[64,15,256]{2,0,1:T(8,128)S(1)} collective-permute-done((f32[64,15,256]{2,0,1:T(8,128)S(1)}, f32[64,15,256]{2,0,1:T(8,128)S(1)}, u32[]{:S(2)}, u32[]{:S(2)}) %collective-permute-start.13) | collective-permute-done | bytes 983072 | tf_op jit(solution)/shard_map/ppermute | solution.py:15
  655.9 16.7 %bitcast_divide_fusion = f32[128,64,256]{2,0,1:T(8,128)S(1)} fusion(f32[1,128,64,256]{3,2,1,0:T(8,128)} %param.3, f32[158,64,256]{2,1,0:T(8,128)S(1)} %pad_maximum_fusion.1, f32[128,158]{0,1:T(8,128)S(1)} %copy-done.9), kind=kOutput, calls=%fused_computation.6 | convolution fusion | flops 1990197248 | bytes 27212800 | tf_op jit(solution)/shard_map/pi,ijk->pjk/dot_general | solution.py:71
  673.4 13.2 %collective-permute-start.18 = (f32[15,64,256]{2,1,0:T(8,128)S(1)}, f32[15,64,256]{2,1,0:T(8,128)S(1)}, u32[]{:S(2)}, u32[]{:S(2)}) collective-permute-start(f32[15,64,256]{2,1,0:T(8,128)S(1)} %copy.61), channel_id=1, source_target_pairs={{0,8},{8,16},{16,24},{1,9},{9,17},{17,25},{2,10},{10,18},{18,26},{... | collective-permute-start | bytes 2949128 | tf_op jit(solution)/shard_map/ppermute | solution.py:14
  698.0 10.3 %collective-permute-done.19 = f32[64,15,256]{2,0,1:T(8,128)S(1)} collective-permute-done((f32[64,15,256]{2,0,1:T(8,128)S(1)}, f32[64,15,256]{2,0,1:T(8,128)S(1)}, u32[]{:S(2)}, u32[]{:S(2)}) %collective-permute-start.19) | collective-permute-done | bytes 983072 | tf_op jit(solution)/shard_map/ppermute | solution.py:14
  713.8 5.8 fusion.38
  725.7 12.6 %collective-permute-done.21 = f32[15,64,256]{2,1,0:T(8,128)S(1)} collective-permute-done((f32[15,64,256]{2,1,0:T(8,128)S(1)}, f32[15,64,256]{2,1,0:T(8,128)S(1)}, u32[]{:S(2)}, u32[]{:S(2)}) %collective-permute-start.21) | collective-permute-done | bytes 983072 | tf_op jit(solution)/shard_map/ppermute | solution.py:15
  746.9 10.2 %collective-permute-done.22 = f32[64,15,256]{2,0,1:T(8,128)S(1)} collective-permute-done((f32[64,15,256]{2,0,1:T(8,128)S(1)}, f32[64,15,256]{2,0,1:T(8,128)S(1)}, u32[]{:S(2)}, u32[]{:S(2)}) %collective-permute-start.22) | collective-permute-done | bytes 983072 | tf_op jit(solution)/shard_map/ppermute | solution.py:14
  772.0 38.1 %reduce-scatter.9.cloned.1.call-done = f32[64,16,256]{2,1,0:T(8,128)} async-done(((f32[64,64,256]{2,1,0:T(8,128)}), f32[64,16,256]{2,1,0:T(8,128)}) %reduce-scatter.9.cloned.1.call-update) | async-done | bytes 1048592 | tf_op jit(solution)/shard_map/reduce_scatter | solution.py:84
  811.5 78.2 %reduce-scatter.11.cloned.1.call-done = f32[64,16,256]{2,1,0:T(8,128)} async-done(((f32[64,64,256]{2,1,0:T(8,128)}), f32[64,16,256]{2,1,0:T(8,128)}) %reduce-scatter.11.cloned.1.call-update) | async-done | bytes 1048592 | tf_op jit(solution)/shard_map/reduce_scatter | solution.py:84
  (150 shorter events, 180.0 us)
Async XLA Ops:
  6.5 86.7 %all-gather.5.cloned.1.call-start = ((), (), s32[]{:S(2)}) async-start(), calls=%async_computation.4 | async-start | bytes 5242880 | tf_op jit(solution)/shard_map/all_gather | solution.py:66
  9.6 164.5 %all-gather.7.cloned.1.call-start = ((), (), s32[]{:S(2)}) async-start(), calls=%async_computation.5 | async-start | bytes 5242880 | tf_op jit(solution)/shard_map/all_gather | solution.py:66
  93.3 276.2 %reduce-scatter.5.cloned.1.call-start = ((), (), s32[]{:S(2)}) async-start(), calls=%async_computation.6 | async-start | bytes 5242880 | tf_op jit(solution)/shard_map/reduce_scatter | solution.py:84
  97.4 86.1 %collective-permute-start.4 = (f32[64,15,256]{2,0,1:T(8,128)}, f32[64,15,256]{2,0,1:T(8,128)}, u32[]{:S(2)}, u32[]{:S(2)}) collective-permute-start(f32[64,15,256]{2,0,1:T(8,128)} %copy.41), channel_id=1, source_target_pairs={{4,0},{5,1},{6,2},{7,3},{12,8},{13,9},{14,10},{15,11},{20,16},{21,... | collective-permute-start | bytes 2949128 | tf_op jit(solution)/shard_map/ppermute | solution.py:15
  98.7 86.6 %collective-permute-start.3 = (f32[64,15,256]{2,0,1:T(8,128)S(1)}, f32[64,15,256]{2,0,1:T(8,128)}, u32[]{:S(2)}, u32[]{:S(2)}) collective-permute-start(f32[64,15,256]{2,0,1:T(8,128)S(1)} %copy.40), channel_id=1, source_target_pairs={{0,4},{1,5},{2,6},{3,7},{8,12},{9,13},{10,14},{11,15},{16,20},{17,... | collective-permute-start | bytes 2949128 | tf_op jit(solution)/shard_map/ppermute | solution.py:14
  177.2 25.4 %collective-permute-start.1 = (f32[64,15,256]{2,0,1:T(8,128)S(1)}, f32[64,15,256]{2,0,1:T(8,128)S(1)}, u32[]{:S(2)}, u32[]{:S(2)}) collective-permute-start(f32[64,15,256]{2,0,1:T(8,128)S(1)} %copy.37), channel_id=1, source_target_pairs={{4,0},{5,1},{6,2},{7,3},{12,8},{13,9},{14,10},{15,11},{20,16},{21,... | collective-permute-start | bytes 2949128 | tf_op jit(solution)/shard_map/ppermute | solution.py:15
  178.5 25.3 %collective-permute-start = (f32[64,15,256]{2,0,1:T(8,128)S(1)}, f32[64,15,256]{2,0,1:T(8,128)S(1)}, u32[]{:S(2)}, u32[]{:S(2)}) collective-permute-start(f32[64,15,256]{2,0,1:T(8,128)S(1)} %copy.36), channel_id=1, source_target_pairs={{0,4},{1,5},{2,6},{3,7},{8,12},{9,13},{10,14},{11,15},{16,20},{17,... | collective-permute-start | bytes 2949128 | tf_op jit(solution)/shard_map/ppermute | solution.py:14
  192.2 19.8 %collective-permute-start.5 = (f32[15,64,256]{2,1,0:T(8,128)S(1)}, f32[15,64,256]{2,1,0:T(8,128)S(1)}, u32[]{:S(2)}, u32[]{:S(2)}) collective-permute-start(f32[15,64,256]{2,1,0:T(8,128)S(1)} %slice.155), channel_id=1, source_target_pairs={{8,0},{16,8},{24,16},{9,1},{17,9},{25,17},{10,2},{18,10},{26,18},{... | collective-permute-start | bytes 2949128 | tf_op jit(solution)/shard_map/ppermute | solution.py:93
  251.7 16.1 %collective-permute-start.7 = (f32[64,15,256]{2,0,1:T(8,128)S(1)}, f32[64,15,256]{2,0,1:T(8,128)S(1)}, u32[]{:S(2)}, u32[]{:S(2)}) collective-permute-start(f32[64,15,256]{2,0,1:T(8,128)S(1)} %get-tuple-element.31), channel_id=1, source_target_pairs={{0,4},{1,5},{2,6},{3,7},{8,12},{9,13},{10,14},{11,15},{16,20},{17,... | collective-permute-start | bytes 2949128 | tf_op jit(solution)/shard_map/ppermute | solution.py:14
  256.1 16.4 %collective-permute-start.8 = (f32[64,15,256]{2,0,1:T(8,128)S(1)}, f32[64,15,256]{2,0,1:T(8,128)S(1)}, u32[]{:S(2)}, u32[]{:S(2)}) collective-permute-start(f32[64,15,256]{2,0,1:T(8,128)S(1)} %get-tuple-element.32), channel_id=1, source_target_pairs={{4,0},{5,1},{6,2},{7,3},{12,8},{13,9},{14,10},{15,11},{20,16},{21,... | collective-permute-start | bytes 2949128 | tf_op jit(solution)/shard_map/ppermute | solution.py:15
  283.0 166.0 %reduce-scatter.7.cloned.1.call-start = ((), (), s32[]{:S(2)}) async-start(), calls=%async_computation.7 | async-start | bytes 5242880 | tf_op jit(solution)/shard_map/reduce_scatter | solution.py:84
  304.9 16.0 %collective-permute-start.11 = (f32[64,15,256]{2,0,1:T(8,128)S(1)}, f32[64,15,256]{2,0,1:T(8,128)S(1)}, u32[]{:S(2)}, u32[]{:S(2)}) collective-permute-start(f32[64,15,256]{2,0,1:T(8,128)S(1)} %get-tuple-element.34), channel_id=1, source_target_pairs={{4,0},{5,1},{6,2},{7,3},{12,8},{13,9},{14,10},{15,11},{20,16},{21,... | collective-permute-start | bytes 2949128 | tf_op jit(solution)/shard_map/ppermute | solution.py:15
  369.5 164.3 %all-gather.9.cloned.1.call-start = ((), (), s32[]{:S(2)}) async-start(), calls=%async_computation.8 | async-start | bytes 5242880 | tf_op jit(solution)/shard_map/all_gather | solution.py:66
  452.4 162.2 %all-gather.11.cloned.1.call-start = ((), (), s32[]{:S(2)}) async-start(), calls=%async_computation.9 | async-start | bytes 5242880 | tf_op jit(solution)/shard_map/all_gather | solution.py:66
  533.8 276.2 %reduce-scatter.9.cloned.1.call-start = ((), (), s32[]{:S(2)}) async-start(), calls=%async_computation.10 | async-start | bytes 5242880 | tf_op jit(solution)/shard_map/reduce_scatter | solution.py:84
  536.4 87.2 %collective-permute-start.16 = (f32[64,15,256]{2,0,1:T(8,128)S(1)}, f32[64,15,256]{2,0,1:T(8,128)S(1)}, u32[]{:S(2)}, u32[]{:S(2)}) collective-permute-start(f32[64,15,256]{2,0,1:T(8,128)S(1)} %copy.57), channel_id=1, source_target_pairs={{4,0},{5,1},{6,2},{7,3},{12,8},{13,9},{14,10},{15,11},{20,16},{21,... | collective-permute-start | bytes 2949128 | tf_op jit(solution)/shard_map/ppermute | solution.py:15
  539.2 85.0 %collective-permute-start.15 = (f32[64,15,256]{2,0,1:T(8,128)}, f32[64,15,256]{2,0,1:T(8,128)}, u32[]{:S(2)}, u32[]{:S(2)}) collective-permute-start(f32[64,15,256]{2,0,1:T(8,128)} %copy.56), channel_id=1, source_target_pairs={{0,4},{1,5},{2,6},{3,7},{8,12},{9,13},{10,14},{11,15},{16,20},{17,... | collective-permute-start | bytes 2949128 | tf_op jit(solution)/shard_map/ppermute | solution.py:14
  617.0 25.4 %collective-permute-start.13 = (f32[64,15,256]{2,0,1:T(8,128)S(1)}, f32[64,15,256]{2,0,1:T(8,128)S(1)}, u32[]{:S(2)}, u32[]{:S(2)}) collective-permute-start(f32[64,15,256]{2,0,1:T(8,128)S(1)} %copy.53), channel_id=1, source_target_pairs={{4,0},{5,1},{6,2},{7,3},{12,8},{13,9},{14,10},{15,11},{20,16},{21,... | collective-permute-start | bytes 2949128 | tf_op jit(solution)/shard_map/ppermute | solution.py:15
  618.9 25.3 %collective-permute-start.12 = (f32[64,15,256]{2,0,1:T(8,128)S(1)}, f32[64,15,256]{2,0,1:T(8,128)S(1)}, u32[]{:S(2)}, u32[]{:S(2)}) collective-permute-start(f32[64,15,256]{2,0,1:T(8,128)S(1)} %copy.52), channel_id=1, source_target_pairs={{0,4},{1,5},{2,6},{3,7},{8,12},{9,13},{10,14},{11,15},{16,20},{17,... | collective-permute-start | bytes 2949128 | tf_op jit(solution)/shard_map/ppermute | solution.py:14
  631.1 20.7 %collective-permute-start.17 = (f32[15,64,256]{2,1,0:T(8,128)S(1)}, f32[15,64,256]{2,1,0:T(8,128)S(1)}, u32[]{:S(2)}, u32[]{:S(2)}) collective-permute-start(f32[15,64,256]{2,1,0:T(8,128)S(1)} %slice.168), channel_id=1, source_target_pairs={{8,0},{16,8},{24,16},{9,1},{17,9},{25,17},{10,2},{18,10},{26,18},{... | collective-permute-start | bytes 2949128 | tf_op jit(solution)/shard_map/ppermute | solution.py:93
  692.2 16.1 %collective-permute-start.19 = (f32[64,15,256]{2,0,1:T(8,128)S(1)}, f32[64,15,256]{2,0,1:T(8,128)S(1)}, u32[]{:S(2)}, u32[]{:S(2)}) collective-permute-start(f32[64,15,256]{2,0,1:T(8,128)S(1)} %get-tuple-element.23), channel_id=1, source_target_pairs={{0,4},{1,5},{2,6},{3,7},{8,12},{9,13},{10,14},{11,15},{16,20},{17,... | collective-permute-start | bytes 2949128 | tf_op jit(solution)/shard_map/ppermute | solution.py:14
  696.7 16.4 %collective-permute-start.20 = (f32[64,15,256]{2,0,1:T(8,128)S(1)}, f32[64,15,256]{2,0,1:T(8,128)S(1)}, u32[]{:S(2)}, u32[]{:S(2)}) collective-permute-start(f32[64,15,256]{2,0,1:T(8,128)S(1)} %get-tuple-element.24), channel_id=1, source_target_pairs={{4,0},{5,1},{6,2},{7,3},{12,8},{13,9},{14,10},{15,11},{20,16},{21,... | collective-permute-start | bytes 2949128 | tf_op jit(solution)/shard_map/ppermute | solution.py:15
  723.6 166.2 %reduce-scatter.11.cloned.1.call-start = ((), (), s32[]{:S(2)}) async-start(), calls=%async_computation.11 | async-start | bytes 5242880 | tf_op jit(solution)/shard_map/reduce_scatter | solution.py:84
  745.5 16.0 %collective-permute-start.23 = (f32[64,15,256]{2,0,1:T(8,128)S(1)}, f32[64,15,256]{2,0,1:T(8,128)S(1)}, u32[]{:S(2)}, u32[]{:S(2)}) collective-permute-start(f32[64,15,256]{2,0,1:T(8,128)S(1)} %get-tuple-element.26), channel_id=1, source_target_pairs={{4,0},{5,1},{6,2},{7,3},{12,8},{13,9},{14,10},{15,11},{20,16},{21,... | collective-permute-start | bytes 2949128 | tf_op jit(solution)/shard_map/ppermute | solution.py:15
  (19 other events, 562.0 us)
Sparse Core Ops, SparseCore 0:
  9.7 83.4 all-gather.4
  94.8 79.2 all-gather.6
  283.1 86.3 reduce-scatter.4
  371.7 77.2 reduce-scatter.6
  452.5 81.2 all-gather.8
  535.2 79.2 all-gather.10
  723.7 86.3 reduce-scatter.8
  812.4 77.2 reduce-scatter.10

commit v2 on v0

v2 whole, which is shorter than its diff:
```python
import jax
import jax.numpy as jnp
from jax import lax
from jax.sharding import PartitionSpec as P

ITERS = 2


def swap(last, first, axis):
    size = lax.axis_size(axis)
    before = lax.ppermute(last, axis, [(i, i + 1) for i in range(size - 1)])
    behind = lax.ppermute(first, axis, [(i + 1, i) for i in range(size - 1)])
    return before, behind


def band(kernel, out_size, in_size, shift_cells, adjoint):
    half_width = (kernel.shape[0] - 1) // 2
    out_index = lax.broadcasted_iota(jnp.int32, (out_size, in_size), 0)
    in_index = lax.broadcasted_iota(jnp.int32, (out_size, in_size), 1)
    offset_cells = in_index - out_index + shift_cells
    if adjoint:
        tap_index = half_width + offset_cells
    else:
        tap_index = half_width - offset_cells
    choose = tap_index[:, :, None] == lax.broadcasted_iota(jnp.int32, (1, 1, kernel.shape[0]), 2)
    return jnp.sum(jnp.where(choose, kernel, jnp.zeros_like(kernel)), axis=2)


def after(x, done):
    return x + 0.0 * done[0, 0, 0]


def body(recorded, psf_taps, estimate):
    m = (psf_taps.shape[2] - 1) // 2
    view_count = psf_taps.shape[0] * lax.axis_size("vert")
    kernels = psf_taps[0] / jnp.sum(psf_taps[0], axis=1, keepdims=True)
    view_data = recorded[0]
    bx, bz, by = view_data.shape
    e = bx // 4
    high = lax.Precision.HIGH
    mats = []
    for adjoint in (False, True):
        mats.append((
            band(kernels[0], bx, bx + 2 * m, -m, adjoint),
            band(kernels[1], bz, bz + 2 * m, -m, adjoint),
            band(kernels[2], by, by, 0, adjoint),
        ))
    (fx, fz, fy), (ax, az, ay) = mats

    def dims12(piece, zmat, ymat, done=None):
        length = piece.shape[1]
        low, high_rows = piece[:, :m], piece[:, length - m:]
        if done is not None:
            low, high_rows = after(low, done), after(high_rows, done)
        before, behind = swap(high_rows, low, "gy")
        wide = jnp.concatenate([before, piece, behind], axis=1)
        out = jnp.einsum("qj,pjk->pqk", zmat, wide, precision=high)
        return jnp.einsum("pqk,rk->pqr", out, ymat, precision=high)

    def along_x(mat, wide):
        return jnp.einsum("pi,ijk->pjk", mat, wide, precision=high)

    def gather(x):
        return lax.all_gather(x, "vert", axis=1, tiled=True)

    def scatter(x):
        return lax.psum_scatter(x, "vert", scatter_dimension=1, tiled=True)

    own_edge = jnp.concatenate([estimate[:e], estimate[bx - e:]], axis=0)
    own_mid = estimate[e:bx - e]
    for iteration in range(ITERS):
        edge = gather(own_edge)
        own_mid, edge = lax.optimization_barrier((own_mid, edge))
        mid = gather(own_mid)
        edge = dims12(edge, fz, fy)
        before, behind = swap(edge[2 * e - m:], edge[:m], "gx")
        mid = dims12(mid, fz, fy, edge)
        wide = jnp.concatenate([before, edge[:e], mid, edge[e:], behind], axis=0)
        ratio = view_data / along_x(fx, wide)
        part = along_x(ax[e:bx - e, e:bx - e + 2 * m], ratio[e - m:bx - e + m])
        corr_mid = dims12(part, az, ay)
        sum_mid = scatter(corr_mid)
        before, behind = swap(after(ratio[bx - m:], corr_mid), after(ratio[:m], corr_mid), "gx")
        low = jnp.concatenate([before, ratio[:e + m]], axis=0)
        upper = jnp.concatenate([ratio[bx - e - m:], behind], axis=0)
        part = jnp.concatenate([
            along_x(ax[:e, :e + 2 * m], low),
            along_x(ax[bx - e:, bx - e:], upper),
        ], axis=0)
        corr_edge = dims12(part, az, ay)
        sum_edge = scatter(corr_edge)
        own_mid = own_mid * (sum_mid / view_count)
        own_edge = own_edge * (sum_edge / view_count)
    return jnp.concatenate([own_edge[:e], own_mid, own_edge[e:]], axis=0)


def solution(mesh):
    in_specs = (P("vert", "gx", "gy", None), P("vert", None, None), P("gx", ("gy", "vert"), None))
    out_specs = P("gx", ("gy", "vert"), None)
    return jax.shard_map(body, mesh=mesh, in_specs=in_specs, out_specs=out_specs, check_vma=False)
```

time: 1120 us -> 1040 us (0.929)
  waiting for transfers between devices: 798 us -> 634 us
  local copies, waits for them, and re-layouts: 21.5 us -> 167 us
  matrix products: 219 us -> 116 us
  other arithmetic: 13.7 us -> 50.9 us
    dot_general x12 -> x24, matrix products: 219 us -> 116 us  [the longest x8 48.8 us: along_x(): return jnp.einsum('pi,ijk->pjk', mat, wide, precision=high)]
    concatenate x0 -> x3, local copies, waits for them, and re-layouts: none -> 94.8 us  [the longest x2 93.2 us: body(): wide = jnp.concatenate([before, edge[:e], mid, edge[e:], behind], axis=0)]
    all_gather x2 -> x4, waiting for transfers between devices: 303 us -> 237 us  [gather(): return lax.all_gather(x, 'vert', axis=1, tiled=True)]
    ppermute x16 -> x24, waiting for transfers between devices: 194 us -> 131 us  [the longest x12 98.4 us: swap(): before = lax.ppermute(last, axis, [(i, i + 1) for i in range(size - 1)])]
    reduce_scatter x2 -> x4, waiting for transfers between devices: 301 us -> 266 us  [scatter(): return lax.psum_scatter(x, 'vert', scatter_dimension=1, tiled=True)]
    div x0 -> x2, other arithmetic: none -> 28.3 us  [body(): ratio = view_data / along_x(fx, wide)]
    slice x12 -> x25, local copies, waits for them, and re-layouts: 8.71 us -> 35.9 us  [the longest x6 11.8 us: body(): wide = jnp.concatenate([before, edge[:e], mid, edge[e:], behind], axis=0)]
    ppermute x16 -> x24, starting transfers between devices: 51.8 us -> 45.3 us  [the longest x12 27.2 us: swap(): before = lax.ppermute(last, axis, [(i, i + 1) for i in range(size - 1)])]
  transfers between devices with their start and end apart: 20 -> 32, of which waited for: 16 -> 25; matrix products, arithmetic and copies ran while one was open for 1% -> 10% of each run, Pallas kernels for 0% -> 0%
where the time goes in v2:
time: 1040 us; the launch traced here: 1030 us
  waiting for transfers between devices  634 us (61%)
  local copies, waits for them, and re-layouts  167 us (16%)
  matrix products  116 us (11%)
  other arithmetic  50.9 us (5%)
  starting transfers between devices  45.6 us (4%)
  between operations  16.9 us (2%)
    reduce_scatter x4, waiting for transfers between devices, scatter(): return lax.psum_scatter(x, 'vert', scatter_dimension=1, tiled=True)  266 us
    all_gather x4, waiting for transfers between devices, gather(): return lax.all_gather(x, 'vert', axis=1, tiled=True)  237 us
    ppermute x12, waiting for transfers between devices, swap(): before = lax.ppermute(last, axis, [(i, i + 1) for i in range(size - 1)])  98.4 us
    concatenate x2, local copies, waits for them, and re-layouts, body(): wide = jnp.concatenate([before, edge[:e], mid, edge[e:], behind], axis=0)  93.2 us
    dot_general x8, matrix products, along_x(): return jnp.einsum('pi,ijk->pjk', mat, wide, precision=high)  48.8 us
    dot_general x8, matrix products, dims12(): out = jnp.einsum('qj,pjk->pqk', zmat, wide, precision=high)  35.4 us
    ppermute x12, waiting for transfers between devices, swap(): behind = lax.ppermute(first, axis, [(i + 1, i) for i in range(size - 1)])  32.3 us
    dot_general x8, matrix products, dims12(): return jnp.einsum('pqk,rk->pqr', out, ymat, precision=high)  31.7 us
  transfers between devices with their start and end apart: 32, of which 25 were waited for; matrix products, arithmetic and copies ran while one was open for 10% of the time, Pallas kernels for 0%

profile of v2, /device:TPU:0, one launch (start us, length us, event | category | flops | bytes accessed | tf_op | source)
XLA Modules:
  0.0 1029.7 jit_solution(5927430110584675160)
XLA Ops:
  10.7 83.5 %all-gather.5.cloned.1.call-done = f32[64,64,256]{2,0,1:T(8,128)} async-done(((f32[64,16,256]{2,0,1:T(8,128)}), f32[64,64,256]{2,0,1:T(8,128)}) %all-gather.5.cloned.1.call-update) | async-done | bytes 4194320 | tf_op jit(solution)/shard_map/all_gather | solution.py:64
  107.5 14.8 %collective-permute-done = f32[64,15,256]{2,0,1:T(8,128)S(1)} collective-permute-done((f32[64,15,256]{2,0,1:T(8,128)S(1)}, f32[64,15,256]{2,0,1:T(8,128)S(1)}, u32[]{:S(2)}, u32[]{:S(2)}) %collective-permute-start) | collective-permute-done | bytes 983072 | tf_op jit(solution)/shard_map/ppermute | solution.py:11
  139.6 35.6 %all-gather.7.cloned.1.call-done = f32[64,64,256]{2,0,1:T(8,128)} async-done(((f32[64,16,256]{2,0,1:T(8,128)}), f32[64,64,256]{2,0,1:T(8,128)}) %all-gather.7.cloned.1.call-update) | async-done | bytes 4194320 | tf_op jit(solution)/shard_map/all_gather | solution.py:64
  209.3 6.2 fusion.58
  215.5 46.2 %concatenate.57 = f32[158,64,256]{2,0,1:T(8,128)} concatenate(f32[15,64,256]{2,0,1:T(8,128)} %copy.135, f32[32,64,256]{2,0,1:T(8,128)S(1)} %copy.136, f32[64,64,256]{2,0,1:T(8,128)} %fusion.58, f32[32,64,256]{2,0,1:T(8,128)} %copy.137, f32[15,64,256]{2,0,1:T(8,128)} %copy.138), dimensions={0} | concatenate | bytes 20709376 | tf_op jit(solution)/shard_map/concatenate | solution.py:78
  261.7 11.6 %fusion.78 = f32[128,64,256]{2,0,1:T(8,128)} fusion(f32[158,64,256]{2,0,1:T(8,128)} %concatenate.57, f32[128,158]{0,1:T(8,128)} %get-tuple-element.18), kind=kOutput, calls=%fused_computation.115 | convolution fusion | flops 1988100096 | bytes 18824192 | tf_op jit(solution)/shard_map/pi,ijk->pjk/dot_general | solution.py:61
  273.2 14.1 %bitcast_divide_fusion.1 = f32[128,64,256]{2,1,0:T(8,128)} fusion(f32[1,128,64,256]{3,2,1,0:T(8,128)} %param.3, f32[128,64,256]{2,0,1:T(8,128)} %fusion.78), kind=kLoop, calls=%fused_computation.1 | loop fusion | flops 2097152 | bytes 25165824 | tf_op jit(solution)/shard_map/div | solution.py:79
  290.1 5.9 fusion.34
  299.0 18.5 %collective-permute-done.6 = f32[64,15,256]{2,0,1:T(8,128)S(1)} collective-permute-done((f32[64,15,256]{2,0,1:T(8,128)S(1)}, f32[64,15,256]{2,0,1:T(8,128)S(1)}, u32[]{:S(2)}, u32[]{:S(2)}) %collective-permute-start.6) | collective-permute-done | bytes 983072 | tf_op jit(solution)/shard_map/ppermute | solution.py:11
  353.0 12.8 %collective-permute-done.10 = f32[64,15,256]{2,0,1:T(8,128)S(1)} collective-permute-done((f32[64,15,256]{2,0,1:T(8,128)S(1)}, f32[64,15,256]{2,0,1:T(8,128)S(1)}, u32[]{:S(2)}, u32[]{:S(2)}) %collective-permute-start.10) | collective-permute-done | bytes 983072 | tf_op jit(solution)/shard_map/ppermute | solution.py:11
  381.6 82.4 %reduce-scatter.5.cloned.1.call-done = f32[64,16,256]{2,1,0:T(8,128)} async-done(((f32[64,64,256]{2,1,0:T(8,128)}), f32[64,16,256]{2,1,0:T(8,128)}) %reduce-scatter.5.cloned.1.call-update) | async-done | bytes 1048592 | tf_op jit(solution)/shard_map/reduce_scatter | solution.py:67
  467.2 76.4 %reduce-scatter.7.cloned.1.call-done = f32[64,16,256]{2,1,0:T(8,128)} async-done(((f32[64,64,256]{2,1,0:T(8,128)}), f32[64,16,256]{2,1,0:T(8,128)}) %reduce-scatter.7.cloned.1.call-update) | async-done | bytes 1048592 | tf_op jit(solution)/shard_map/reduce_scatter | solution.py:67
  545.1 81.3 %all-gather.9.cloned.1.call-done = f32[64,64,256]{2,0,1:T(8,128)} async-done(((f32[64,16,256]{2,0,1:T(8,128)}), f32[64,64,256]{2,0,1:T(8,128)}) %all-gather.9.cloned.1.call-update) | async-done | bytes 4194320 | tf_op jit(solution)/shard_map/all_gather | solution.py:64
  639.6 14.5 %collective-permute-done.12 = f32[64,15,256]{2,0,1:T(8,128)S(1)} collective-permute-done((f32[64,15,256]{2,0,1:T(8,128)S(1)}, f32[64,15,256]{2,0,1:T(8,128)S(1)}, u32[]{:S(2)}, u32[]{:S(2)}) %collective-permute-start.12) | collective-permute-done | bytes 983072 | tf_op jit(solution)/shard_map/ppermute | solution.py:11
  670.8 36.6 %all-gather.11.cloned.1.call-done = f32[64,64,256]{2,0,1:T(8,128)} async-done(((f32[64,16,256]{2,0,1:T(8,128)}), f32[64,64,256]{2,0,1:T(8,128)}) %all-gather.11.cloned.1.call-update) | async-done | bytes 4194320 | tf_op jit(solution)/shard_map/all_gather | solution.py:64
  741.3 6.2 fusion.52
  747.5 47.0 %concatenate.65 = f32[158,64,256]{2,0,1:T(8,128)} concatenate(f32[15,64,256]{2,0,1:T(8,128)} %copy.156, f32[32,64,256]{2,0,1:T(8,128)} %copy.157, f32[64,64,256]{2,0,1:T(8,128)} %fusion.52, f32[32,64,256]{2,0,1:T(8,128)} %copy.158, f32[15,64,256]{2,0,1:T(8,128)} %copy.159), dimensions={0} | concatenate | bytes 20709376 | tf_op jit(solution)/shard_map/concatenate | solution.py:78
  794.5 11.5 %fusion.76 = f32[128,64,256]{2,0,1:T(8,128)} fusion(f32[158,64,256]{2,0,1:T(8,128)} %concatenate.65, f32[128,158]{0,1:T(8,128)S(1)} %copy-done.14), kind=kOutput, calls=%fused_computation.113 | convolution fusion | flops 1988100096 | bytes 18824192 | tf_op jit(solution)/shard_map/pi,ijk->pjk/dot_general | solution.py:61
  806.0 14.1 %bitcast_divide_fusion = f32[128,64,256]{2,1,0:T(8,128)} fusion(f32[1,128,64,256]{3,2,1,0:T(8,128)} %param.3, f32[128,64,256]{2,0,1:T(8,128)} %fusion.76), kind=kLoop, calls=%fused_computation | loop fusion | flops 2097152 | bytes 25165824 | tf_op jit(solution)/shard_map/div | solution.py:79
  822.9 5.9 fusion.28
  831.8 18.5 %collective-permute-done.18 = f32[64,15,256]{2,0,1:T(8,128)S(1)} collective-permute-done((f32[64,15,256]{2,0,1:T(8,128)S(1)}, f32[64,15,256]{2,0,1:T(8,128)S(1)}, u32[]{:S(2)}, u32[]{:S(2)}) %collective-permute-start.18) | collective-permute-done | bytes 983072 | tf_op jit(solution)/shard_map/ppermute | solution.py:11
  886.5 10.1 collective-permute-done.22
  911.4 28.5 %reduce-scatter.11.cloned.1.call-done = f32[64,16,256]{2,1,0:T(8,128)} async-done(((f32[64,64,256]{2,1,0:T(8,128)}), f32[64,16,256]{2,1,0:T(8,128)}) %reduce-scatter.11.cloned.1.call-update) | async-done | bytes 1048592 | tf_op jit(solution)/shard_map/reduce_scatter | solution.py:67
  941.4 78.2 %reduce-scatter.9.cloned.1.call-done = f32[64,16,256]{2,1,0:T(8,128)} async-done(((f32[64,64,256]{2,1,0:T(8,128)}), f32[64,16,256]{2,1,0:T(8,128)}) %reduce-scatter.9.cloned.1.call-update) | async-done | bytes 1048592 | tf_op jit(solution)/shard_map/reduce_scatter | solution.py:67
  (182 shorter events, 252.5 us)
Async XLA Ops:
  6.5 87.6 %all-gather.5.cloned.1.call-start = ((), (), s32[]{:S(2)}) async-start(), calls=%async_computation.4 | async-start | bytes 5242880 | tf_op jit(solution)/shard_map/all_gather | solution.py:64
  10.6 164.7 %all-gather.7.cloned.1.call-start = ((), (), s32[]{:S(2)}) async-start(), calls=%async_computation.5 | async-start | bytes 5242880 | tf_op jit(solution)/shard_map/all_gather | solution.py:64
  95.8 368.3 %reduce-scatter.5.cloned.1.call-start = ((), (), s32[]{:S(2)}) async-start(), calls=%async_computation.6 | async-start | bytes 5242880 | tf_op jit(solution)/shard_map/reduce_scatter | solution.py:67
  97.9 24.4 %collective-permute-start = (f32[64,15,256]{2,0,1:T(8,128)S(1)}, f32[64,15,256]{2,0,1:T(8,128)S(1)}, u32[]{:S(2)}, u32[]{:S(2)}) collective-permute-start(f32[64,15,256]{2,0,1:T(8,128)S(1)} %get-tuple-element.49), channel_id=1, source_target_pairs={{0,4},{1,5},{2,6},{3,7},{8,12},{9,13},{10,14},{11,15},{16,20},{17,... | collective-permute-start | bytes 2949128 | tf_op jit(solution)/shard_map/ppermute | solution.py:11
  101.4 25.1 %collective-permute-start.1 = (f32[64,15,256]{2,0,1:T(8,128)S(1)}, f32[64,15,256]{2,0,1:T(8,128)S(1)}, u32[]{:S(2)}, u32[]{:S(2)}) collective-permute-start(f32[64,15,256]{2,0,1:T(8,128)S(1)} %get-tuple-element.50), channel_id=1, source_target_pairs={{4,0},{5,1},{6,2},{7,3},{12,8},{13,9},{14,10},{15,11},{20,16},{21,... | collective-permute-start | bytes 2949128 | tf_op jit(solution)/shard_map/ppermute | solution.py:12
  135.5 52.4 %collective-permute-start.2 = (f32[15,64,256]{2,1,0:T(8,128)}, f32[15,64,256]{2,1,0:T(8,128)}, u32[]{:S(2)}, u32[]{:S(2)}) collective-permute-start(f32[15,64,256]{2,1,0:T(8,128)} %get-tuple-element.44), channel_id=1, source_target_pairs={{0,8},{8,16},{16,24},{1,9},{9,17},{17,25},{2,10},{10,18},{18,26},{... | collective-permute-start | bytes 2949128 | tf_op jit(solution)/shard_map/ppermute | solution.py:11
  137.8 53.0 %collective-permute-start.5 = (f32[15,64,256]{2,1,0:T(8,128)}, f32[15,64,256]{2,1,0:T(8,128)}, u32[]{:S(2)}, u32[]{:S(2)}) collective-permute-start(f32[15,64,256]{2,1,0:T(8,128)} %get-tuple-element.43), channel_id=1, source_target_pairs={{8,0},{16,8},{24,16},{9,1},{17,9},{25,17},{10,2},{18,10},{26,18},{... | collective-permute-start | bytes 2949128 | tf_op jit(solution)/shard_map/ppermute | solution.py:12
  177.1 24.4 %collective-permute-start.3 = (f32[64,15,256]{2,0,1:T(8,128)S(1)}, f32[64,15,256]{2,0,1:T(8,128)S(1)}, u32[]{:S(2)}, u32[]{:S(2)}) collective-permute-start(f32[64,15,256]{2,0,1:T(8,128)S(1)} %get-tuple-element.47), channel_id=1, source_target_pairs={{0,4},{1,5},{2,6},{3,7},{8,12},{9,13},{10,14},{11,15},{16,20},{17,... | collective-permute-start | bytes 2949128 | tf_op jit(solution)/shard_map/ppermute | solution.py:11
  180.6 25.1 %collective-permute-start.4 = (f32[64,15,256]{2,0,1:T(8,128)S(1)}, f32[64,15,256]{2,0,1:T(8,128)S(1)}, u32[]{:S(2)}, u32[]{:S(2)}) collective-permute-start(f32[64,15,256]{2,0,1:T(8,128)S(1)} %get-tuple-element.48), channel_id=1, source_target_pairs={{4,0},{5,1},{6,2},{7,3},{12,8},{13,9},{14,10},{15,11},{20,16},{21,... | collective-permute-start | bytes 2949128 | tf_op jit(solution)/shard_map/ppermute | solution.py:12
  296.2 21.3 %collective-permute-start.6 = (f32[64,15,256]{2,0,1:T(8,128)S(1)}, f32[64,15,256]{2,0,1:T(8,128)S(1)}, u32[]{:S(2)}, u32[]{:S(2)}) collective-permute-start(f32[64,15,256]{2,0,1:T(8,128)S(1)} %get-tuple-element.41), channel_id=1, source_target_pairs={{0,4},{1,5},{2,6},{3,7},{8,12},{9,13},{10,14},{11,15},{16,20},{17,... | collective-permute-start | bytes 2949128 | tf_op jit(solution)/shard_map/ppermute | solution.py:11
  297.7 24.0 %collective-permute-start.7 = (f32[64,15,256]{2,0,1:T(8,128)S(1)}, f32[64,15,256]{2,0,1:T(8,128)S(1)}, u32[]{:S(2)}, u32[]{:S(2)}) collective-permute-start(f32[64,15,256]{2,0,1:T(8,128)S(1)} %get-tuple-element.42), channel_id=1, source_target_pairs={{4,0},{5,1},{6,2},{7,3},{12,8},{13,9},{14,10},{15,11},{20,16},{21,... | collective-permute-start | bytes 2949128 | tf_op jit(solution)/shard_map/ppermute | solution.py:12
  381.0 162.6 %reduce-scatter.7.cloned.1.call-start = ((), (), s32[]{:S(2)}) async-start(), calls=%async_computation.7 | async-start | bytes 5242880 | tf_op jit(solution)/shard_map/reduce_scatter | solution.py:67
  381.6 244.7 %all-gather.9.cloned.1.call-start = ((), (), s32[]{:S(2)}) async-start(), calls=%async_computation.8 | async-start | bytes 5242880 | tf_op jit(solution)/shard_map/all_gather | solution.py:64
  467.1 240.3 %all-gather.11.cloned.1.call-start = ((), (), s32[]{:S(2)}) async-start(), calls=%async_computation.9 | async-start | bytes 5242880 | tf_op jit(solution)/shard_map/all_gather | solution.py:64
  627.9 312.0 %reduce-scatter.11.cloned.1.call-start = ((), (), s32[]{:S(2)}) async-start(), calls=%async_computation.11 | async-start | bytes 5242880 | tf_op jit(solution)/shard_map/reduce_scatter | solution.py:67
  629.7 24.4 %collective-permute-start.12 = (f32[64,15,256]{2,0,1:T(8,128)S(1)}, f32[64,15,256]{2,0,1:T(8,128)S(1)}, u32[]{:S(2)}, u32[]{:S(2)}) collective-permute-start(f32[64,15,256]{2,0,1:T(8,128)S(1)} %get-tuple-element.37), channel_id=1, source_target_pairs={{0,4},{1,5},{2,6},{3,7},{8,12},{9,13},{10,14},{11,15},{16,20},{17,... | collective-permute-start | bytes 2949128 | tf_op jit(solution)/shard_map/ppermute | solution.py:11
  633.1 25.1 %collective-permute-start.13 = (f32[64,15,256]{2,0,1:T(8,128)S(1)}, f32[64,15,256]{2,0,1:T(8,128)S(1)}, u32[]{:S(2)}, u32[]{:S(2)}) collective-permute-start(f32[64,15,256]{2,0,1:T(8,128)S(1)} %get-tuple-element.38), channel_id=1, source_target_pairs={{4,0},{5,1},{6,2},{7,3},{12,8},{13,9},{14,10},{15,11},{20,16},{21,... | collective-permute-start | bytes 2949128 | tf_op jit(solution)/shard_map/ppermute | solution.py:12
  667.2 54.6 %collective-permute-start.14 = (f32[15,64,256]{2,1,0:T(8,128)}, f32[15,64,256]{2,1,0:T(8,128)}, u32[]{:S(2)}, u32[]{:S(2)}) collective-permute-start(f32[15,64,256]{2,1,0:T(8,128)} %get-tuple-element.32), channel_id=1, source_target_pairs={{0,8},{8,16},{16,24},{1,9},{9,17},{17,25},{2,10},{10,18},{18,26},{... | collective-permute-start | bytes 2949128 | tf_op jit(solution)/shard_map/ppermute | solution.py:11
  669.5 55.1 %collective-permute-start.17 = (f32[15,64,256]{2,1,0:T(8,128)}, f32[15,64,256]{2,1,0:T(8,128)}, u32[]{:S(2)}, u32[]{:S(2)}) collective-permute-start(f32[15,64,256]{2,1,0:T(8,128)} %get-tuple-element.31), channel_id=1, source_target_pairs={{8,0},{16,8},{24,16},{9,1},{17,9},{25,17},{10,2},{18,10},{26,18},{... | collective-permute-start | bytes 2949128 | tf_op jit(solution)/shard_map/ppermute | solution.py:12
  709.1 24.4 %collective-permute-start.15 = (f32[64,15,256]{2,0,1:T(8,128)S(1)}, f32[64,15,256]{2,0,1:T(8,128)S(1)}, u32[]{:S(2)}, u32[]{:S(2)}) collective-permute-start(f32[64,15,256]{2,0,1:T(8,128)S(1)} %get-tuple-element.35), channel_id=1, source_target_pairs={{0,4},{1,5},{2,6},{3,7},{8,12},{9,13},{10,14},{11,15},{16,20},{17,... | collective-permute-start | bytes 2949128 | tf_op jit(solution)/shard_map/ppermute | solution.py:11
  712.6 25.1 %collective-permute-start.16 = (f32[64,15,256]{2,0,1:T(8,128)S(1)}, f32[64,15,256]{2,0,1:T(8,128)S(1)}, u32[]{:S(2)}, u32[]{:S(2)}) collective-permute-start(f32[64,15,256]{2,0,1:T(8,128)S(1)} %get-tuple-element.36), channel_id=1, source_target_pairs={{4,0},{5,1},{6,2},{7,3},{12,8},{13,9},{14,10},{15,11},{20,16},{21,... | collective-permute-start | bytes 2949128 | tf_op jit(solution)/shard_map/ppermute | solution.py:12
  828.9 21.3 %collective-permute-start.18 = (f32[64,15,256]{2,0,1:T(8,128)S(1)}, f32[64,15,256]{2,0,1:T(8,128)S(1)}, u32[]{:S(2)}, u32[]{:S(2)}) collective-permute-start(f32[64,15,256]{2,0,1:T(8,128)S(1)} %get-tuple-element.29), channel_id=1, source_target_pairs={{0,4},{1,5},{2,6},{3,7},{8,12},{9,13},{10,14},{11,15},{16,20},{17,... | collective-permute-start | bytes 2949128 | tf_op jit(solution)/shard_map/ppermute | solution.py:11
  830.5 24.0 %collective-permute-start.19 = (f32[64,15,256]{2,0,1:T(8,128)S(1)}, f32[64,15,256]{2,0,1:T(8,128)S(1)}, u32[]{:S(2)}, u32[]{:S(2)}) collective-permute-start(f32[64,15,256]{2,0,1:T(8,128)S(1)} %get-tuple-element.30), channel_id=1, source_target_pairs={{4,0},{5,1},{6,2},{7,3},{12,8},{13,9},{14,10},{15,11},{20,16},{21,... | collective-permute-start | bytes 2949128 | tf_op jit(solution)/shard_map/ppermute | solution.py:12
  865.0 154.6 %reduce-scatter.9.cloned.1.call-start = ((), (), s32[]{:S(2)}) async-start(), calls=%async_computation.10 | async-start | bytes 5242880 | tf_op jit(solution)/shard_map/reduce_scatter | solution.py:67
  (26 other events, 472.4 us)
Sparse Core Ops, SparseCore 0:
  10.7 83.4 all-gather.4
  95.9 79.2 all-gather.6
  381.1 82.8 reduce-scatter.4
  466.3 77.2 reduce-scatter.6
  545.0 81.2 all-gather.8
  628.0 79.2 all-gather.10
  865.1 74.7 reduce-scatter.10
  942.3 77.2 reduce-scatter.8

commit v3 on v2

--- a/solution.py
+++ b/solution.py
@@ -46,6 +46,11 @@
             band(kernels[2], by, by, 0, adjoint),
         ))
     (fx, fz, fy), (ax, az, ay) = mats
+    h = -(-m // 8) * 8
+    fx = band(kernels[0], bx, bx + 2 * h, -h, False)
+    fx = jnp.concatenate([
+        fx[:, h:h + e], fx[:, h + bx - e:h + bx], fx[:, h + e:h + bx - e], fx[:, :h], fx[:, h + bx:],
+    ], axis=1)
 
     def dims12(piece, zmat, ymat, done=None):
         length = piece.shape[1]
@@ -73,9 +78,9 @@
         own_mid, edge = lax.optimization_barrier((own_mid, edge))
         mid = gather(own_mid)
         edge = dims12(edge, fz, fy)
-        before, behind = swap(edge[2 * e - m:], edge[:m], "gx")
+        before, behind = swap(edge[2 * e - h:], edge[:h], "gx")
         mid = dims12(mid, fz, fy, edge)
-        wide = jnp.concatenate([before, edge[:e], mid, edge[e:], behind], axis=0)
+        wide = jnp.concatenate([edge, mid, before, behind], axis=0)
         ratio = view_data / along_x(fx, wide)
         part = along_x(ax[e:bx - e, e:bx - e + 2 * m], ratio[e - m:bx - e + m])
         corr_mid = dims12(part, az, ay)
@@ -88,6 +93,7 @@
             along_x(ax[bx - e:, bx - e:], upper),
         ], axis=0)
         corr_edge = dims12(part, az, ay)
+        sum_mid, corr_edge = lax.optimization_barrier((sum_mid, corr_edge))
         sum_edge = scatter(corr_edge)
         own_mid = own_mid * (sum_mid / view_count)
         own_edge = own_edge * (sum_edge / view_count)

time: 1040 us -> 878 us (0.84)
  local copies, waits for them, and re-layouts: 167 us -> 54.1 us
  waiting for transfers between devices: 634 us -> 598 us
  matrix products: 116 us -> 105 us
    concatenate x2 -> x1, local copies, waits for them, and re-layouts: 93.2 us -> 0.01 us  [body(): jnp.concatenate([fx[:, h:h + e], fx[:, h + bx - e:h + bx], fx[:, h + e:h...]
    reduce_scatter x4, waiting for transfers between devices: 266 us -> 215 us  [scatter(): return lax.psum_scatter(x, 'vert', scatter_dimension=1, tiled=True)]
    ppermute x12, waiting for transfers between devices: 32.3 us -> 43.8 us  [swap(): behind = lax.ppermute(first, axis, [(i + 1, i) for i in range(size - 1)])]
    slice x8 -> x2, local copies, waits for them, and re-layouts: 14.6 us -> 3.52 us  [body(): before, behind = swap(edge[2 * e - h:], edge[:h], 'gx')]
  transfers between devices with their start and end apart: 32 -> 32, of which waited for: 25 -> 26; matrix products, arithmetic and copies ran while one was open for 10% -> 12% of each run, Pallas kernels for 0% -> 0%
where the time goes in v3:
time: 878 us; the launch traced here: 874 us
  waiting for transfers between devices  598 us (68%)
  matrix products  105 us (12%)
  local copies, waits for them, and re-layouts  54.1 us (6%)
  other arithmetic  53.9 us (6%)
  starting transfers between devices  45.9 us (5%)
  between operations  17.2 us (2%)
    all_gather x4, waiting for transfers between devices, gather(): return lax.all_gather(x, 'vert', axis=1, tiled=True)  243 us
    reduce_scatter x4, waiting for transfers between devices, scatter(): return lax.psum_scatter(x, 'vert', scatter_dimension=1, tiled=True)  215 us
    ppermute x12, waiting for transfers between devices, swap(): before = lax.ppermute(last, axis, [(i, i + 1) for i in range(size - 1)])  95.8 us
    dot_general x8, matrix products, along_x(): return jnp.einsum('pi,ijk->pjk', mat, wide, precision=high)  47 us
    ppermute x12, waiting for transfers between devices, swap(): behind = lax.ppermute(first, axis, [(i + 1, i) for i in range(size - 1)])  43.8 us
    dot_general x8, matrix products, dims12(): out = jnp.einsum('qj,pjk->pqk', zmat, wide, precision=high)  35.4 us
    div x2, other arithmetic, body(): ratio = view_data / along_x(fx, wide)  28.2 us
    ppermute x12, starting transfers between devices, swap(): before = lax.ppermute(last, axis, [(i, i + 1) for i in range(size - 1)])  27.4 us
  transfers between devices with their start and end apart: 32, of which 26 were waited for; matrix products, arithmetic and copies ran while one was open for 12% of the time, Pallas kernels for 0%

profile of v3, /device:TPU:0, one launch (start us, length us, event | category | flops | bytes accessed | tf_op | source)
XLA Modules:
  0.0 874.4 jit_solution(17080999530562400410)
XLA Ops:
  10.9 82.3 %all-gather.5.cloned.1.call-done = f32[64,64,256]{2,0,1:T(8,128)} async-done(((f32[64,16,256]{2,0,1:T(8,128)}), f32[64,64,256]{2,0,1:T(8,128)}) %all-gather.5.cloned.1.call-update) | async-done | bytes 4194320 | tf_op jit(solution)/shard_map/all_gather | solution.py:69
  108.2 15.0 %collective-permute-done.1 = f32[64,15,256]{2,0,1:T(8,128)S(1)} collective-permute-done((f32[64,15,256]{2,0,1:T(8,128)S(1)}, f32[64,15,256]{2,0,1:T(8,128)S(1)}, u32[]{:S(2)}, u32[]{:S(2)}) %collective-permute-start.1) | collective-permute-done | bytes 983072 | tf_op jit(solution)/shard_map/ppermute | solution.py:12
  133.2 41.0 %all-gather.7.cloned.1.call-done = f32[64,64,256]{2,0,1:T(8,128)} async-done(((f32[64,16,256]{2,0,1:T(8,128)}), f32[64,64,256]{2,0,1:T(8,128)}) %all-gather.7.cloned.1.call-update) | async-done | bytes 4194320 | tf_op jit(solution)/shard_map/all_gather | solution.py:69
  188.9 11.7 %collective-permute-done.2 = f32[64,15,256]{2,0,1:T(8,128)S(1)} collective-permute-done((f32[64,15,256]{2,0,1:T(8,128)S(1)}, f32[64,15,256]{2,0,1:T(8,128)S(1)}, u32[]{:S(2)}, u32[]{:S(2)}) %collective-permute-start.2) | collective-permute-done | bytes 983072 | tf_op jit(solution)/shard_map/ppermute | solution.py:11
  212.3 10.9 %fusion.2 = f32[128,64,256]{2,0,1:T(8,128)} fusion(f32[160,64,256]{2,1,0:T(8,128)S(1)} %pad_maximum_fusion, f32[128,160]{0,1:T(8,128)S(1)} %constant_dynamic-update-slice_fusion), kind=kOutput, calls=%fused_computation.4 | convolution fusion | flops 2013265920 | bytes 18956288 | tf_op jit(solution)/shard_map/pi,ijk->pjk/dot_general | solution.py:66
  223.2 14.1 %bitcast_divide_fusion.1 = f32[128,64,256]{2,1,0:T(8,128)} fusion(f32[1,128,64,256]{3,2,1,0:T(8,128)} %param.3, f32[128,64,256]{2,0,1:T(8,128)} %fusion.2), kind=kLoop, calls=%fused_computation.7 | loop fusion | flops 2097152 | bytes 25165824 | tf_op jit(solution)/shard_map/div | solution.py:84
  249.0 18.3 %collective-permute-done.6 = f32[64,15,256]{2,0,1:T(8,128)S(1)} collective-permute-done((f32[64,15,256]{2,0,1:T(8,128)S(1)}, f32[64,15,256]{2,0,1:T(8,128)S(1)}, u32[]{:S(2)}, u32[]{:S(2)}) %collective-permute-start.6) | collective-permute-done | bytes 983072 | tf_op jit(solution)/shard_map/ppermute | solution.py:11
  272.2 5.8 fusion.36
  303.5 10.1 %collective-permute-done.10 = f32[64,15,256]{2,0,1:T(8,128)S(1)} collective-permute-done((f32[64,15,256]{2,0,1:T(8,128)S(1)}, f32[64,15,256]{2,0,1:T(8,128)S(1)}, u32[]{:S(2)}, u32[]{:S(2)}) %collective-permute-start.10) | collective-permute-done | bytes 983072 | tf_op jit(solution)/shard_map/ppermute | solution.py:11
  318.8 5.8 fusion.34
  328.4 28.5 %reduce-scatter.5.cloned.1.call-done = f32[64,16,256]{2,1,0:T(8,128)} async-done(((f32[64,64,256]{2,1,0:T(8,128)}), f32[64,16,256]{2,1,0:T(8,128)}) %reduce-scatter.5.cloned.1.call-update) | async-done | bytes 1048592 | tf_op jit(solution)/shard_map/reduce_scatter | solution.py:72
  357.0 79.5 %reduce-scatter.7.cloned.1.call-done = f32[64,16,256]{2,1,0:T(8,128)} async-done(((f32[64,64,256]{2,1,0:T(8,128)}), f32[64,16,256]{2,1,0:T(8,128)}) %reduce-scatter.7.cloned.1.call-update) | async-done | bytes 1048592 | tf_op jit(solution)/shard_map/reduce_scatter | solution.py:72
  441.0 79.9 %all-gather.9.cloned.1.call-done = f32[64,64,256]{2,0,1:T(8,128)} async-done(((f32[64,16,256]{2,0,1:T(8,128)}), f32[64,64,256]{2,0,1:T(8,128)}) %all-gather.9.cloned.1.call-update) | async-done | bytes 4194320 | tf_op jit(solution)/shard_map/all_gather | solution.py:69
  534.1 14.5 %collective-permute-done.12 = f32[64,15,256]{2,0,1:T(8,128)S(1)} collective-permute-done((f32[64,15,256]{2,0,1:T(8,128)S(1)}, f32[64,15,256]{2,0,1:T(8,128)S(1)}, u32[]{:S(2)}, u32[]{:S(2)}) %collective-permute-start.12) | collective-permute-done | bytes 983072 | tf_op jit(solution)/shard_map/ppermute | solution.py:11
  561.6 40.3 %all-gather.11.cloned.1.call-done = f32[64,64,256]{2,0,1:T(8,128)} async-done(((f32[64,16,256]{2,0,1:T(8,128)}), f32[64,64,256]{2,0,1:T(8,128)}) %all-gather.11.cloned.1.call-update) | async-done | bytes 4194320 | tf_op jit(solution)/shard_map/all_gather | solution.py:69
  616.1 12.2 %collective-permute-done.14 = f32[64,15,256]{2,0,1:T(8,128)S(1)} collective-permute-done((f32[64,15,256]{2,0,1:T(8,128)S(1)}, f32[64,15,256]{2,0,1:T(8,128)S(1)}, u32[]{:S(2)}, u32[]{:S(2)}) %collective-permute-start.14) | collective-permute-done | bytes 983072 | tf_op jit(solution)/shard_map/ppermute | solution.py:11
  640.1 10.9 %fusion = f32[128,64,256]{2,0,1:T(8,128)} fusion(f32[160,64,256]{2,1,0:T(8,128)S(1)} %pad_maximum_fusion.1, f32[128,160]{0,1:T(8,128)S(1)} %copy-done.10), kind=kOutput, calls=%fused_computation.2 | convolution fusion | flops 2013265920 | bytes 18956288 | tf_op jit(solution)/shard_map/pi,ijk->pjk/dot_general | solution.py:66
  651.0 14.1 %bitcast_divide_fusion = f32[128,64,256]{2,1,0:T(8,128)} fusion(f32[1,128,64,256]{3,2,1,0:T(8,128)} %param.3, f32[128,64,256]{2,0,1:T(8,128)} %fusion), kind=kLoop, calls=%fused_computation.6 | loop fusion | flops 2097152 | bytes 25165824 | tf_op jit(solution)/shard_map/div | solution.py:84
  676.7 18.3 %collective-permute-done.18 = f32[64,15,256]{2,0,1:T(8,128)S(1)} collective-permute-done((f32[64,15,256]{2,0,1:T(8,128)S(1)}, f32[64,15,256]{2,0,1:T(8,128)S(1)}, u32[]{:S(2)}, u32[]{:S(2)}) %collective-permute-start.18) | collective-permute-done | bytes 983072 | tf_op jit(solution)/shard_map/ppermute | solution.py:11
  700.0 5.8 fusion.30
  731.2 10.1 %collective-permute-done.22 = f32[64,15,256]{2,0,1:T(8,128)S(1)} collective-permute-done((f32[64,15,256]{2,0,1:T(8,128)S(1)}, f32[64,15,256]{2,0,1:T(8,128)S(1)}, u32[]{:S(2)}, u32[]{:S(2)}) %collective-permute-start.22) | collective-permute-done | bytes 983072 | tf_op jit(solution)/shard_map/ppermute | solution.py:11
  746.5 5.8 fusion.28
  756.1 28.5 %reduce-scatter.9.cloned.1.call-done = f32[64,16,256]{2,1,0:T(8,128)} async-done(((f32[64,64,256]{2,1,0:T(8,128)}), f32[64,16,256]{2,1,0:T(8,128)}) %reduce-scatter.9.cloned.1.call-update) | async-done | bytes 1048592 | tf_op jit(solution)/shard_map/reduce_scatter | solution.py:72
  786.1 78.2 %reduce-scatter.11.cloned.1.call-done = f32[64,16,256]{2,1,0:T(8,128)} async-done(((f32[64,64,256]{2,1,0:T(8,128)}), f32[64,16,256]{2,1,0:T(8,128)}) %reduce-scatter.11.cloned.1.call-update) | async-done | bytes 1048592 | tf_op jit(solution)/shard_map/reduce_scatter | solution.py:72
  (171 shorter events, 215.9 us)
Async XLA Ops:
  6.5 86.6 %all-gather.5.cloned.1.call-start = ((), (), s32[]{:S(2)}) async-start(), calls=%async_computation.4 | async-start | bytes 5242880 | tf_op jit(solution)/shard_map/all_gather | solution.py:69
  9.5 164.7 %all-gather.7.cloned.1.call-start = ((), (), s32[]{:S(2)}) async-start(), calls=%async_computation.5 | async-start | bytes 5242880 | tf_op jit(solution)/shard_map/all_gather | solution.py:69
  94.7 262.2 %reduce-scatter.5.cloned.1.call-start = ((), (), s32[]{:S(2)}) async-start(), calls=%async_computation.6 | async-start | bytes 5242880 | tf_op jit(solution)/shard_map/reduce_scatter | solution.py:72
  97.8 25.4 %collective-permute-start.1 = (f32[64,15,256]{2,0,1:T(8,128)S(1)}, f32[64,15,256]{2,0,1:T(8,128)S(1)}, u32[]{:S(2)}, u32[]{:S(2)}) collective-permute-start(f32[64,15,256]{2,0,1:T(8,128)S(1)} %get-tuple-element.52), channel_id=1, source_target_pairs={{4,0},{5,1},{6,2},{7,3},{12,8},{13,9},{14,10},{15,11},{20,16},{21,... | collective-permute-start | bytes 2949128 | tf_op jit(solution)/shard_map/ppermute | solution.py:12
  99.1 25.3 %collective-permute-start = (f32[64,15,256]{2,0,1:T(8,128)S(1)}, f32[64,15,256]{2,0,1:T(8,128)S(1)}, u32[]{:S(2)}, u32[]{:S(2)}) collective-permute-start(f32[64,15,256]{2,0,1:T(8,128)S(1)} %get-tuple-element.51), channel_id=1, source_target_pairs={{0,4},{1,5},{2,6},{3,7},{8,12},{9,13},{10,14},{11,15},{16,20},{17,... | collective-permute-start | bytes 2949128 | tf_op jit(solution)/shard_map/ppermute | solution.py:11
  176.0 24.5 %collective-permute-start.2 = (f32[64,15,256]{2,0,1:T(8,128)S(1)}, f32[64,15,256]{2,0,1:T(8,128)S(1)}, u32[]{:S(2)}, u32[]{:S(2)}) collective-permute-start(f32[64,15,256]{2,0,1:T(8,128)S(1)} %get-tuple-element.47), channel_id=1, source_target_pairs={{0,4},{1,5},{2,6},{3,7},{8,12},{9,13},{10,14},{11,15},{16,20},{17,... | collective-permute-start | bytes 2949128 | tf_op jit(solution)/shard_map/ppermute | solution.py:11
  179.6 25.1 %collective-permute-start.3 = (f32[64,15,256]{2,0,1:T(8,128)S(1)}, f32[64,15,256]{2,0,1:T(8,128)S(1)}, u32[]{:S(2)}, u32[]{:S(2)}) collective-permute-start(f32[64,15,256]{2,0,1:T(8,128)S(1)} %get-tuple-element.48), channel_id=1, source_target_pairs={{4,0},{5,1},{6,2},{7,3},{12,8},{13,9},{14,10},{15,11},{20,16},{21,... | collective-permute-start | bytes 2949128 | tf_op jit(solution)/shard_map/ppermute | solution.py:12
  182.7 27.5 %collective-permute-start.4 = (f32[16,64,256]{2,1,0:T(8,128)S(1)}, f32[16,64,256]{2,1,0:T(8,128)S(1)}, u32[]{:S(2)}, u32[]{:S(2)}) collective-permute-start(f32[16,64,256]{2,1,0:T(8,128)S(1)} %get-tuple-element.49), channel_id=1, source_target_pairs={{0,8},{8,16},{16,24},{1,9},{9,17},{17,25},{2,10},{10,18},{18,26},{... | collective-permute-start | bytes 3145736 | tf_op jit(solution)/shard_map/ppermute | solution.py:11
  184.2 26.0 %collective-permute-start.5 = (f32[16,64,256]{2,1,0:T(8,128)S(1)}, f32[16,64,256]{2,1,0:T(8,128)S(1)}, u32[]{:S(2)}, u32[]{:S(2)}) collective-permute-start(f32[16,64,256]{2,1,0:T(8,128)S(1)} %get-tuple-element.50), channel_id=1, source_target_pairs={{8,0},{16,8},{24,16},{9,1},{17,9},{25,17},{10,2},{18,10},{26,18},{... | collective-permute-start | bytes 3145736 | tf_op jit(solution)/shard_map/ppermute | solution.py:12
  245.9 21.3 %collective-permute-start.6 = (f32[64,15,256]{2,0,1:T(8,128)S(1)}, f32[64,15,256]{2,0,1:T(8,128)S(1)}, u32[]{:S(2)}, u32[]{:S(2)}) collective-permute-start(f32[64,15,256]{2,0,1:T(8,128)S(1)} %get-tuple-element.45), channel_id=1, source_target_pairs={{0,4},{1,5},{2,6},{3,7},{8,12},{9,13},{10,14},{11,15},{16,20},{17,... | collective-permute-start | bytes 2949128 | tf_op jit(solution)/shard_map/ppermute | solution.py:11
  247.5 24.0 %collective-permute-start.7 = (f32[64,15,256]{2,0,1:T(8,128)S(1)}, f32[64,15,256]{2,0,1:T(8,128)S(1)}, u32[]{:S(2)}, u32[]{:S(2)}) collective-permute-start(f32[64,15,256]{2,0,1:T(8,128)S(1)} %get-tuple-element.46), channel_id=1, source_target_pairs={{4,0},{5,1},{6,2},{7,3},{12,8},{13,9},{14,10},{15,11},{20,16},{21,... | collective-permute-start | bytes 2949128 | tf_op jit(solution)/shard_map/ppermute | solution.py:12
  282.0 154.5 %reduce-scatter.7.cloned.1.call-start = ((), (), s32[]{:S(2)}) async-start(), calls=%async_computation.7 | async-start | bytes 5242880 | tf_op jit(solution)/shard_map/reduce_scatter | solution.py:72
  356.9 164.0 %all-gather.9.cloned.1.call-start = ((), (), s32[]{:S(2)}) async-start(), calls=%async_computation.8 | async-start | bytes 5242880 | tf_op jit(solution)/shard_map/all_gather | solution.py:69
  439.5 162.5 %all-gather.11.cloned.1.call-start = ((), (), s32[]{:S(2)}) async-start(), calls=%async_computation.9 | async-start | bytes 5242880 | tf_op jit(solution)/shard_map/all_gather | solution.py:69
  522.5 262.1 %reduce-scatter.9.cloned.1.call-start = ((), (), s32[]{:S(2)}) async-start(), calls=%async_computation.10 | async-start | bytes 5242880 | tf_op jit(solution)/shard_map/reduce_scatter | solution.py:72
  524.2 24.4 %collective-permute-start.12 = (f32[64,15,256]{2,0,1:T(8,128)S(1)}, f32[64,15,256]{2,0,1:T(8,128)S(1)}, u32[]{:S(2)}, u32[]{:S(2)}) collective-permute-start(f32[64,15,256]{2,0,1:T(8,128)S(1)} %get-tuple-element.41), channel_id=1, source_target_pairs={{0,4},{1,5},{2,6},{3,7},{8,12},{9,13},{10,14},{11,15},{16,20},{17,... | collective-permute-start | bytes 2949128 | tf_op jit(solution)/shard_map/ppermute | solution.py:11
  527.7 25.1 %collective-permute-start.13 = (f32[64,15,256]{2,0,1:T(8,128)S(1)}, f32[64,15,256]{2,0,1:T(8,128)S(1)}, u32[]{:S(2)}, u32[]{:S(2)}) collective-permute-start(f32[64,15,256]{2,0,1:T(8,128)S(1)} %get-tuple-element.42), channel_id=1, source_target_pairs={{4,0},{5,1},{6,2},{7,3},{12,8},{13,9},{14,10},{15,11},{20,16},{21,... | collective-permute-start | bytes 2949128 | tf_op jit(solution)/shard_map/ppermute | solution.py:12
  603.8 24.5 %collective-permute-start.14 = (f32[64,15,256]{2,0,1:T(8,128)S(1)}, f32[64,15,256]{2,0,1:T(8,128)S(1)}, u32[]{:S(2)}, u32[]{:S(2)}) collective-permute-start(f32[64,15,256]{2,0,1:T(8,128)S(1)} %get-tuple-element.37), channel_id=1, source_target_pairs={{0,4},{1,5},{2,6},{3,7},{8,12},{9,13},{10,14},{11,15},{16,20},{17,... | collective-permute-start | bytes 2949128 | tf_op jit(solution)/shard_map/ppermute | solution.py:11
  607.4 25.1 %collective-permute-start.15 = (f32[64,15,256]{2,0,1:T(8,128)S(1)}, f32[64,15,256]{2,0,1:T(8,128)S(1)}, u32[]{:S(2)}, u32[]{:S(2)}) collective-permute-start(f32[64,15,256]{2,0,1:T(8,128)S(1)} %get-tuple-element.38), channel_id=1, source_target_pairs={{4,0},{5,1},{6,2},{7,3},{12,8},{13,9},{14,10},{15,11},{20,16},{21,... | collective-permute-start | bytes 2949128 | tf_op jit(solution)/shard_map/ppermute | solution.py:12
  610.5 27.6 %collective-permute-start.16 = (f32[16,64,256]{2,1,0:T(8,128)S(1)}, f32[16,64,256]{2,1,0:T(8,128)S(1)}, u32[]{:S(2)}, u32[]{:S(2)}) collective-permute-start(f32[16,64,256]{2,1,0:T(8,128)S(1)} %get-tuple-element.39), channel_id=1, source_target_pairs={{0,8},{8,16},{16,24},{1,9},{9,17},{17,25},{2,10},{10,18},{18,26},{... | collective-permute-start | bytes 3145736 | tf_op jit(solution)/shard_map/ppermute | solution.py:11
  612.0 26.1 %collective-permute-start.17 = (f32[16,64,256]{2,1,0:T(8,128)S(1)}, f32[16,64,256]{2,1,0:T(8,128)S(1)}, u32[]{:S(2)}, u32[]{:S(2)}) collective-permute-start(f32[16,64,256]{2,1,0:T(8,128)S(1)} %get-tuple-element.40), channel_id=1, source_target_pairs={{8,0},{16,8},{24,16},{9,1},{17,9},{25,17},{10,2},{18,10},{26,18},{... | collective-permute-start | bytes 3145736 | tf_op jit(solution)/shard_map/ppermute | solution.py:12
  673.7 21.3 %collective-permute-start.18 = (f32[64,15,256]{2,0,1:T(8,128)S(1)}, f32[64,15,256]{2,0,1:T(8,128)S(1)}, u32[]{:S(2)}, u32[]{:S(2)}) collective-permute-start(f32[64,15,256]{2,0,1:T(8,128)S(1)} %get-tuple-element.35), channel_id=1, source_target_pairs={{0,4},{1,5},{2,6},{3,7},{8,12},{9,13},{10,14},{11,15},{16,20},{17,... | collective-permute-start | bytes 2949128 | tf_op jit(solution)/shard_map/ppermute | solution.py:11
  675.2 24.0 %collective-permute-start.19 = (f32[64,15,256]{2,0,1:T(8,128)S(1)}, f32[64,15,256]{2,0,1:T(8,128)S(1)}, u32[]{:S(2)}, u32[]{:S(2)}) collective-permute-start(f32[64,15,256]{2,0,1:T(8,128)S(1)} %get-tuple-element.36), channel_id=1, source_target_pairs={{4,0},{5,1},{6,2},{7,3},{12,8},{13,9},{14,10},{15,11},{20,16},{21,... | collective-permute-start | bytes 2949128 | tf_op jit(solution)/shard_map/ppermute | solution.py:12
  709.7 154.6 %reduce-scatter.11.cloned.1.call-start = ((), (), s32[]{:S(2)}) async-start(), calls=%async_computation.11 | async-start | bytes 5242880 | tf_op jit(solution)/shard_map/reduce_scatter | solution.py:72
  (22 other events, 352.8 us)
Sparse Core Ops, SparseCore 0:
  9.6 83.4 all-gather.4
  94.8 79.2 all-gather.6
  282.1 74.7 reduce-scatter.4
  359.1 77.2 reduce-scatter.6
  439.6 81.2 all-gather.8
  522.6 79.2 all-gather.10
  709.8 74.7 reduce-scatter.8
  787.0 77.2 reduce-scatter.10
